TPU v7x, 32 devices: a whole 2x2x4 slice. The times are simulated.
32 devices in a mesh: wide: 16 (over z, y, core), narrow: 2 (over x).
Axes of the slice: x: 2, y: 2, z: 4, core: 2. Of those that a mesh axis runs over, the one named last changes fastest.
Arguments:
- features: bfloat16 [32, 784, 256], P(('wide', 'narrow')), may hold values from -6 to 6
- tag_ids: int32 [32, 512], P(('wide', 'narrow')), may hold values from 0 to 31
- tag_lengths: int32 [32], P(('wide', 'narrow')), may hold values from 22 to 512, as said below
- out_cot: bfloat16 [32, 512, 512], P(('wide', 'narrow')), may hold values from -6 to 6
- proj_weight: bfloat16 [256, 512], P(None, ('wide', 'narrow')), may hold values from -0.375 to 0.375
- bn_given: bfloat16 [2, 512], P(None, ('wide', 'narrow'))
- bn_affine: bfloat16 [2, 512], P(None, ('wide', 'narrow'))
- enc_attn: bfloat16 [4, 512, 512], P(None, ('wide', 'narrow'))
- enc_vec: bfloat16 [5, 512], P(None, ('wide', 'narrow'))
- enc_ffn_in: bfloat16 [512, 1024], P(('wide', 'narrow')), may hold values from -0.25 to 0.25
- enc_hidden_bias: bfloat16 [1024], P(('wide', 'narrow')), may hold values from -4 to 4
- enc_ffn_out: bfloat16 [1024, 512], P(('wide', 'narrow')), may hold values from -0.1875 to 0.1875
- tag_table: bfloat16 [32, 512], P(None, ('wide', 'narrow')), may hold values from -6 to 6
- dec_self: bfloat16 [4, 512, 512], P(None, ('wide', 'narrow'))
- dec_cross: bfloat16 [4, 512, 512], P(None, ('wide', 'narrow'))
- dec_vec: bfloat16 [7, 512], P(None, ('wide', 'narrow'))
- dec_ffn_in: bfloat16 [512, 1024], P(('wide', 'narrow')), may hold values from -0.25 to 0.25
- dec_hidden_bias: bfloat16 [1024], P(('wide', 'narrow')), may hold values from -4 to 4
- dec_ffn_out: bfloat16 [1024, 512], P(('wide', 'narrow')), may hold values from -0.1875 to 0.1875
Outputs:
- decoded: bfloat16 [32, 512, 512], P(('wide', 'narrow'))
- grad_features: float32 [32, 784, 256], P(('wide', 'narrow'))
- grad_proj_weight: float32 [256, 512], P(None, ('wide', 'narrow'))
- grad_bn_affine: float32 [2, 512], P(None, ('wide', 'narrow'))
- grad_enc_attn: float32 [4, 512, 512], P(None, ('wide', 'narrow'))
- grad_enc_vec: float32 [5, 512], P(None, ('wide', 'narrow'))
- grad_enc_ffn_in: float32 [512, 1024], P(('wide', 'narrow'))
- grad_enc_hidden_bias: float32 [1024], P(('wide', 'narrow'))
- grad_enc_ffn_out: float32 [1024, 512], P(('wide', 'narrow'))
- grad_tag_table: float32 [32, 512], P(None, ('wide', 'narrow'))
- grad_dec_self: float32 [4, 512, 512], P(None, ('wide', 'narrow'))
- grad_dec_cross: float32 [4, 512, 512], P(None, ('wide', 'narrow'))
- grad_dec_vec: float32 [7, 512], P(None, ('wide', 'narrow'))
- grad_dec_ffn_in: float32 [512, 1024], P(('wide', 'narrow'))
- grad_dec_hidden_bias: float32 [1024], P(('wide', 'narrow'))
- grad_dec_ffn_out: float32 [1024, 512], P(('wide', 'narrow'))
Inputs may be any that keep to these rules, and one draw needn't show every extreme that they name: `tag_lengths`: one table has exactly 512 tags and one exactly 22.
All inputs are finite; a program needn't handle non-finite values.
Results may differ from a plain program's by a relative error of at most 0.02.
Values may be sent and summed in bfloat16 or wider, within the bound.
A program may use at most 192 MiB of HBM per device.

v0:
```python
from functools import partial
import math

import jax
import jax.numpy as jnp
from jax import lax
from jax.sharding import PartitionSpec as P

HEADS = 8


def product(left, right):
    return jnp.dot(left, right, preferred_element_type=jnp.float32)


def product_inner(left, right):
    return lax.dot_general(
        left, right, (((0,), (0,)), ((), ())), preferred_element_type=jnp.float32
    )


def product_outer(left, right):
    return lax.dot_general(
        left, right, (((1,), (1,)), ((), ())), preferred_element_type=jnp.float32
    )


def positions(row_count, model_width):
    place_index = jnp.arange(row_count, dtype=jnp.float32)[:, None]
    column = jnp.arange(model_width, dtype=jnp.int32)
    inverse = jnp.exp(-(2 * (column // 2)).astype(jnp.float32) / model_width * math.log(10000.0))
    angle_value = place_index * inverse[None, :]
    return jnp.where((column % 2 == 0)[None, :], jnp.sin(angle_value), jnp.cos(angle_value))


def layer_norm(value, gain_row, shift_row):
    centred = value - jnp.mean(value, axis=-1, keepdims=True)
    spread = jnp.mean(centred * centred, axis=-1, keepdims=True)
    return centred * lax.rsqrt(spread + 1e-05) * gain_row + shift_row


def normalize_batch(projected, given_values, affine_values):
    return (projected - given_values[0]) * lax.rsqrt(given_values[1] + 1e-05) * affine_values[
        0
    ] + affine_values[1]


def split_heads(rows_value):
    return rows_value.reshape(rows_value.shape[0], HEADS, -1)


def attend_scores(query_rows, key_rows, allowed):
    heads_query = split_heads(query_rows)
    score_scale = heads_query.shape[2] ** (-0.5)
    raw_scores = jnp.einsum(
        "qhd,khd->hqk", heads_query, split_heads(key_rows), preferred_element_type=jnp.float32
    )
    return (jnp.where(allowed[None], raw_scores * score_scale, -1e30), score_scale)


def attend_forward(query_low, memory_low, weights, allowed):
    query_rows = product(query_low, weights[0]).astype(jnp.bfloat16)
    key_rows = product(memory_low, weights[1]).astype(jnp.bfloat16)
    value_rows = product(memory_low, weights[2]).astype(jnp.bfloat16)
    scores, score_scale = attend_scores(query_rows, key_rows, allowed)
    peak_score = jnp.max(scores, axis=-1, keepdims=True)
    raised = jnp.exp(scores - peak_score)
    row_total = jnp.sum(raised, axis=-1, keepdims=True)
    shares = (raised / row_total).astype(jnp.bfloat16)
    mixed_rows = jnp.einsum(
        "hqk,khd->qhd", shares, split_heads(value_rows), preferred_element_type=jnp.float32
    )
    mixed_rows = mixed_rows.reshape(query_rows.shape).astype(jnp.bfloat16)
    branch = product(mixed_rows, weights[3])
    return (branch, (query_rows, key_rows, value_rows, peak_score + jnp.log(row_total), mixed_rows))


def attend_backward(grad_branch, query_low, memory_low, weights, allowed, stored):
    query_rows, key_rows, value_rows, log_total, mixed_rows = stored
    grad_low = grad_branch.astype(jnp.bfloat16)
    grad_out_weight = product_inner(mixed_rows, grad_low)
    grad_mixed = product_outer(grad_low, weights[3]).astype(jnp.bfloat16)
    scores, score_scale = attend_scores(query_rows, key_rows, allowed)
    shares = jnp.exp(scores - log_total)
    heads_grad = split_heads(grad_mixed)
    grad_value = jnp.einsum(
        "hqk,qhd->khd", shares.astype(jnp.bfloat16), heads_grad, preferred_element_type=jnp.float32
    )
    grad_value = grad_value.reshape(value_rows.shape).astype(jnp.bfloat16)
    grad_shares = jnp.einsum(
        "qhd,khd->hqk", heads_grad, split_heads(value_rows), preferred_element_type=jnp.float32
    )
    inner_sum = jnp.sum(shares * grad_shares, axis=-1, keepdims=True)
    grad_raw = (shares * (grad_shares - inner_sum) * score_scale).astype(jnp.bfloat16)
    grad_query = jnp.einsum(
        "hqk,khd->qhd", grad_raw, split_heads(key_rows), preferred_element_type=jnp.float32
    )
    grad_query = grad_query.reshape(query_rows.shape).astype(jnp.bfloat16)
    grad_key = jnp.einsum(
        "hqk,qhd->khd", grad_raw, split_heads(query_rows), preferred_element_type=jnp.float32
    )
    grad_key = grad_key.reshape(key_rows.shape).astype(jnp.bfloat16)
    weight_grads = jnp.stack(
        [
            product_inner(query_low, grad_query),
            product_inner(memory_low, grad_key),
            product_inner(memory_low, grad_value),
            grad_out_weight,
        ]
    )
    grad_query_in = product_outer(grad_query, weights[0])
    grad_memory_in = product_outer(grad_key, weights[1]) + product_outer(grad_value, weights[2])
    return (grad_query_in, grad_memory_in, weight_grads)


def gelu_exact(value):
    return jax.nn.gelu(value, approximate=False)


def ffn_forward(inputs_low, weight_in, hidden_bias, weight_out, out_bias):
    pre_act = product(inputs_low, weight_in) + hidden_bias.astype(jnp.float32)
    hidden = gelu_exact(pre_act).astype(jnp.bfloat16)
    return (product(hidden, weight_out) + out_bias, (pre_act, hidden))


def ffn_backward(grad_out, inputs_low, weight_in, weight_out, stored):
    pre_act, hidden = stored
    grad_low = grad_out.astype(jnp.bfloat16)
    grad_weight_out = product_inner(hidden, grad_low)
    grad_out_bias = jnp.sum(grad_out, axis=0)
    grad_hidden = product_outer(grad_low, weight_out)
    grad_pre = jax.vjp(gelu_exact, pre_act)[1](grad_hidden)[0]
    grad_pre_low = grad_pre.astype(jnp.bfloat16)
    grad_hidden_bias = jnp.sum(grad_pre, axis=0)
    grad_weight_in = product_inner(inputs_low, grad_pre_low)
    grad_inputs = product_outer(grad_pre_low, weight_in)
    return (grad_inputs, (grad_weight_in, grad_hidden_bias, grad_weight_out, grad_out_bias))


def tag_masks(length_one, tag_count):
    tag_order = jnp.arange(tag_count, dtype=jnp.int32)
    causal = (tag_order[None, :] <= tag_order[:, None]) & (tag_order[None, :] < length_one)
    live_rows = (tag_order < length_one).astype(jnp.float32)[:, None]
    return (causal, live_rows)


def one_hot_rows(ids_one, vocab_size):
    return (ids_one[:, None] == jnp.arange(vocab_size, dtype=jnp.int32)[None, :]).astype(
        jnp.float32
    )


def encoder_forward(weights, features_one):
    proj_weight, bn_given, bn_affine, attn_weights, vectors, ffn_in, hidden_bias, ffn_out = weights
    vector_values = vectors.astype(jnp.float32)
    projected = product(features_one, proj_weight)
    start = normalize_batch(projected, bn_given.astype(jnp.float32), bn_affine.astype(jnp.float32))
    start = start + positions(start.shape[0], start.shape[1])
    start_low = start.astype(jnp.bfloat16)
    all_pairs = jnp.ones((start.shape[0], start.shape[0]), dtype=bool)
    branch, attn_stored = attend_forward(start_low, start_low, attn_weights, all_pairs)
    resid_one = start + branch
    first_out = layer_norm(resid_one, vector_values[0], vector_values[1])
    first_low = first_out.astype(jnp.bfloat16)
    feed_out, ffn_stored = ffn_forward(first_low, ffn_in, hidden_bias, ffn_out, vector_values[2])
    resid_two = first_out + feed_out
    memory = layer_norm(resid_two, vector_values[3], vector_values[4])
    return (
        memory,
        (projected, start_low, resid_one, first_low, resid_two, attn_stored, ffn_stored),
    )


def encoder_backward(weights, features_one, grad_memory, stored):
    proj_weight, bn_given, bn_affine, attn_weights, vectors, ffn_in, hidden_bias, ffn_out = weights
    vector_values = vectors.astype(jnp.float32)
    projected, start_low, resid_one, first_low, resid_two, attn_stored, ffn_stored = stored
    _, back_two = jax.vjp(layer_norm, resid_two, vector_values[3], vector_values[4])
    grad_resid_two, grad_gain_two, grad_shift_two = back_two(grad_memory)
    grad_first_low, ffn_grads = ffn_backward(grad_resid_two, first_low, ffn_in, ffn_out, ffn_stored)
    grad_first = grad_resid_two + grad_first_low
    _, back_one = jax.vjp(layer_norm, resid_one, vector_values[0], vector_values[1])
    grad_resid_one, grad_gain_one, grad_shift_one = back_one(grad_first)
    all_pairs = jnp.ones((start_low.shape[0], start_low.shape[0]), dtype=bool)
    grad_query_in, grad_memory_in, attn_grads = attend_backward(
        grad_resid_one, start_low, start_low, attn_weights, all_pairs, attn_stored
    )
    grad_start = grad_resid_one + grad_query_in + grad_memory_in
    given_values = bn_given.astype(jnp.float32)

    def batch_piece(value, affine_values):
        return normalize_batch(value, given_values, affine_values)

    _, back_norm = jax.vjp(batch_piece, projected, bn_affine.astype(jnp.float32))
    grad_projected, grad_affine = back_norm(grad_start)
    grad_low = grad_projected.astype(jnp.bfloat16)
    grad_proj_weight = product_inner(features_one, grad_low)
    grad_features = product_outer(grad_low, proj_weight)
    grad_weight_in, grad_hidden_bias, grad_weight_out, grad_out_bias = ffn_grads
    grad_vectors = jnp.stack(
        [grad_gain_one, grad_shift_one, grad_out_bias, grad_gain_two, grad_shift_two]
    )
    return (
        (
            grad_proj_weight,
            grad_affine,
            attn_grads,
            grad_vectors,
            grad_weight_in,
            grad_hidden_bias,
            grad_weight_out,
        ),
        grad_features,
    )


def decoder_forward(weights, memory, ids_one, length_one):
    tag_table, self_weights, cross_weights, vectors, ffn_in, hidden_bias, ffn_out = weights
    vector_values = vectors.astype(jnp.float32)
    memory_low = memory.astype(jnp.bfloat16)
    causal, live_rows = tag_masks(length_one, ids_one.shape[0])
    chosen = one_hot_rows(ids_one, tag_table.shape[0])
    embedded = jnp.dot(chosen, tag_table.astype(jnp.float32), precision=lax.Precision.HIGHEST)
    embedded = embedded + positions(embedded.shape[0], embedded.shape[1])
    embedded_low = embedded.astype(jnp.bfloat16)
    branch_self, self_stored = attend_forward(embedded_low, embedded_low, self_weights, causal)
    resid_one = embedded + branch_self
    second = layer_norm(resid_one, vector_values[0], vector_values[1])
    second_low = second.astype(jnp.bfloat16)
    cross_pairs = jnp.ones((ids_one.shape[0], memory.shape[0]), dtype=bool)
    branch_cross, cross_stored = attend_forward(second_low, memory_low, cross_weights, cross_pairs)
    resid_two = second + branch_cross
    third_out = layer_norm(resid_two, vector_values[2], vector_values[3])
    third_low = third_out.astype(jnp.bfloat16)
    feed_out, ffn_stored = ffn_forward(third_low, ffn_in, hidden_bias, ffn_out, vector_values[4])
    resid_three = third_out + feed_out
    last_out = layer_norm(resid_three, vector_values[5], vector_values[6])
    stored = (
        embedded_low,
        resid_one,
        second_low,
        resid_two,
        third_low,
        resid_three,
        self_stored,
        cross_stored,
        ffn_stored,
    )
    return (last_out * live_rows, stored)


def decoder_backward(weights, memory, ids_one, length_one, cot_one, stored):
    tag_table, self_weights, cross_weights, vectors, ffn_in, hidden_bias, ffn_out = weights
    vector_values = vectors.astype(jnp.float32)
    (
        embedded_low,
        resid_one,
        second_low,
        resid_two,
        third_low,
        resid_three,
        self_stored,
        cross_stored,
        ffn_stored,
    ) = stored
    memory_low = memory.astype(jnp.bfloat16)
    causal, live_rows = tag_masks(length_one, ids_one.shape[0])
    cross_pairs = jnp.ones((ids_one.shape[0], memory.shape[0]), dtype=bool)
    _, back_three = jax.vjp(layer_norm, resid_three, vector_values[5], vector_values[6])
    grad_resid_three, grad_gain_three, grad_shift_three = back_three(
        cot_one.astype(jnp.float32) * live_rows
    )
    grad_third_low, ffn_grads = ffn_backward(
        grad_resid_three, third_low, ffn_in, ffn_out, ffn_stored
    )
    grad_third = grad_resid_three + grad_third_low
    _, back_two = jax.vjp(layer_norm, resid_two, vector_values[2], vector_values[3])
    grad_resid_two, grad_gain_two, grad_shift_two = back_two(grad_third)
    grad_second_in, grad_memory, cross_grads = attend_backward(
        grad_resid_two, second_low, memory_low, cross_weights, cross_pairs, cross_stored
    )
    grad_second = grad_resid_two + grad_second_in
    _, back_one = jax.vjp(layer_norm, resid_one, vector_values[0], vector_values[1])
    grad_resid_one, grad_gain_one, grad_shift_one = back_one(grad_second)
    grad_query_in, grad_memory_in, self_grads = attend_backward(
        grad_resid_one, embedded_low, embedded_low, self_weights, causal, self_stored
    )
    grad_embedded = grad_resid_one + grad_query_in + grad_memory_in
    chosen = one_hot_rows(ids_one, tag_table.shape[0])
    grad_table = jnp.dot(chosen.T, grad_embedded, precision=lax.Precision.HIGHEST)
    grad_weight_in, grad_hidden_bias, grad_weight_out, grad_out_bias = ffn_grads
    grad_vectors = jnp.stack(
        [
            grad_gain_one,
            grad_shift_one,
            grad_gain_two,
            grad_shift_two,
            grad_out_bias,
            grad_gain_three,
            grad_shift_three,
        ]
    )
    return (
        (
            grad_table,
            self_grads,
            cross_grads,
            grad_vectors,
            grad_weight_in,
            grad_hidden_bias,
            grad_weight_out,
        ),
        grad_memory,
    )


def zeros_like_all(shapes_from):
    return jax.tree.map(lambda item: jnp.zeros(item.shape, jnp.float32), shapes_from)


def body(
    features,
    tag_ids,
    tag_lengths,
    out_cot,
    proj_weight,
    bn_given,
    bn_affine,
    enc_attn,
    enc_vec,
    enc_ffn_in,
    enc_hidden_bias,
    enc_ffn_out,
    tag_table,
    dec_self,
    dec_cross,
    dec_vec,
    dec_ffn_in,
    dec_hidden_bias,
    dec_ffn_out,
):
    encoder_full = (
        lax.all_gather(proj_weight, ("wide", "narrow"), axis=1, tiled=True),
        lax.all_gather(bn_given, ("wide", "narrow"), axis=1, tiled=True),
        lax.all_gather(bn_affine, ("wide", "narrow"), axis=1, tiled=True),
        lax.all_gather(enc_attn, ("wide", "narrow"), axis=1, tiled=True),
        lax.all_gather(enc_vec, ("wide", "narrow"), axis=1, tiled=True),
        lax.all_gather(enc_ffn_in, ("wide", "narrow"), axis=0, tiled=True),
        lax.all_gather(enc_hidden_bias, ("wide", "narrow"), axis=0, tiled=True),
        lax.all_gather(enc_ffn_out, ("wide", "narrow"), axis=0, tiled=True),
    )
    memories, encoder_stored = lax.map(partial(encoder_forward, encoder_full), features)
    decoder_full = (
        lax.all_gather(tag_table, ("wide", "narrow"), axis=1, tiled=True),
        lax.all_gather(dec_self, ("wide", "narrow"), axis=1, tiled=True),
        lax.all_gather(dec_cross, ("wide", "narrow"), axis=1, tiled=True),
        lax.all_gather(dec_vec, ("wide", "narrow"), axis=1, tiled=True),
        lax.all_gather(dec_ffn_in, ("wide", "narrow"), axis=0, tiled=True),
        lax.all_gather(dec_hidden_bias, ("wide", "narrow"), axis=0, tiled=True),
        lax.all_gather(dec_ffn_out, ("wide", "narrow"), axis=0, tiled=True),
    )

    def decode_one(table_item):
        return decoder_forward(decoder_full, table_item[0], table_item[1], table_item[2])

    decoded_full, decoder_stored = lax.map(decode_one, (memories, tag_ids, tag_lengths))
    decoder_back = (
        lax.all_gather(tag_table, ("wide", "narrow"), axis=1, tiled=True),
        lax.all_gather(dec_self, ("wide", "narrow"), axis=1, tiled=True),
        lax.all_gather(dec_cross, ("wide", "narrow"), axis=1, tiled=True),
        lax.all_gather(dec_vec, ("wide", "narrow"), axis=1, tiled=True),
        lax.all_gather(dec_ffn_in, ("wide", "narrow"), axis=0, tiled=True),
        lax.all_gather(dec_hidden_bias, ("wide", "narrow"), axis=0, tiled=True),
        lax.all_gather(dec_ffn_out, ("wide", "narrow"), axis=0, tiled=True),
    )

    def decoder_step(totals, table_item):
        grads, grad_memory = decoder_backward(
            decoder_back, table_item[0], table_item[1], table_item[2], table_item[3], table_item[4]
        )
        return (jax.tree.map(jnp.add, totals, grads), grad_memory)

    decoder_totals, grad_memories = lax.scan(
        decoder_step,
        zeros_like_all(decoder_back),
        (memories, tag_ids, tag_lengths, out_cot, decoder_stored),
    )
    decoder_shares = (
        lax.psum_scatter(decoder_totals[0], ("wide", "narrow"), scatter_dimension=1, tiled=True),
        lax.psum_scatter(decoder_totals[1], ("wide", "narrow"), scatter_dimension=1, tiled=True),
        lax.psum_scatter(decoder_totals[2], ("wide", "narrow"), scatter_dimension=1, tiled=True),
        lax.psum_scatter(decoder_totals[3], ("wide", "narrow"), scatter_dimension=1, tiled=True),
        lax.psum_scatter(decoder_totals[4], ("wide", "narrow"), scatter_dimension=0, tiled=True),
        lax.psum_scatter(decoder_totals[5], ("wide", "narrow"), scatter_dimension=0, tiled=True),
        lax.psum_scatter(decoder_totals[6], ("wide", "narrow"), scatter_dimension=0, tiled=True),
    )
    encoder_back = (
        lax.all_gather(proj_weight, ("wide", "narrow"), axis=1, tiled=True),
        lax.all_gather(bn_given, ("wide", "narrow"), axis=1, tiled=True),
        lax.all_gather(bn_affine, ("wide", "narrow"), axis=1, tiled=True),
        lax.all_gather(enc_attn, ("wide", "narrow"), axis=1, tiled=True),
        lax.all_gather(enc_vec, ("wide", "narrow"), axis=1, tiled=True),
        lax.all_gather(enc_ffn_in, ("wide", "narrow"), axis=0, tiled=True),
        lax.all_gather(enc_hidden_bias, ("wide", "narrow"), axis=0, tiled=True),
        lax.all_gather(enc_ffn_out, ("wide", "narrow"), axis=0, tiled=True),
    )

    def encoder_step(totals, table_item):
        grads, grad_features = encoder_backward(
            encoder_back, table_item[0], table_item[1], table_item[2]
        )
        return (jax.tree.map(jnp.add, totals, grads), grad_features)

    encoder_zeros = zeros_like_all(
        (
            encoder_back[0],
            encoder_back[2],
            encoder_back[3],
            encoder_back[4],
            encoder_back[5],
            encoder_back[6],
            encoder_back[7],
        )
    )
    encoder_totals, grad_features = lax.scan(
        encoder_step, encoder_zeros, (features, grad_memories, encoder_stored)
    )
    encoder_shares = (
        lax.psum_scatter(encoder_totals[0], ("wide", "narrow"), scatter_dimension=1, tiled=True),
        lax.psum_scatter(encoder_totals[1], ("wide", "narrow"), scatter_dimension=1, tiled=True),
        lax.psum_scatter(encoder_totals[2], ("wide", "narrow"), scatter_dimension=1, tiled=True),
        lax.psum_scatter(encoder_totals[3], ("wide", "narrow"), scatter_dimension=1, tiled=True),
        lax.psum_scatter(encoder_totals[4], ("wide", "narrow"), scatter_dimension=0, tiled=True),
        lax.psum_scatter(encoder_totals[5], ("wide", "narrow"), scatter_dimension=0, tiled=True),
        lax.psum_scatter(encoder_totals[6], ("wide", "narrow"), scatter_dimension=0, tiled=True),
    )
    return (
        decoded_full.astype(jnp.bfloat16),
        grad_features,
        encoder_shares[0],
        encoder_shares[1],
        encoder_shares[2],
        encoder_shares[3],
        encoder_shares[4],
        encoder_shares[5],
        encoder_shares[6],
        decoder_shares[0],
        decoder_shares[1],
        decoder_shares[2],
        decoder_shares[3],
        decoder_shares[4],
        decoder_shares[5],
        decoder_shares[6],
    )


def solution(mesh):
    placed = (
        P(("wide", "narrow"), None, None),
        P(("wide", "narrow"), None),
        P(("wide", "narrow")),
        P(("wide", "narrow"), None, None),
        P(None, ("wide", "narrow")),
        P(None, ("wide", "narrow")),
        P(None, ("wide", "narrow")),
        P(None, ("wide", "narrow"), None),
        P(None, ("wide", "narrow")),
        P(("wide", "narrow"), None),
        P(("wide", "narrow")),
        P(("wide", "narrow"), None),
        P(None, ("wide", "narrow")),
        P(None, ("wide", "narrow"), None),
        P(None, ("wide", "narrow"), None),
        P(None, ("wide", "narrow")),
        P(("wide", "narrow"), None),
        P(("wide", "narrow")),
        P(("wide", "narrow"), None),
    )
    return jax.shard_map(
        body,
        mesh=mesh,
        in_specs=placed,
        out_specs=(
            P(("wide", "narrow"), None, None),
            P(("wide", "narrow"), None, None),
            P(None, ("wide", "narrow")),
            P(None, ("wide", "narrow")),
            P(None, ("wide", "narrow"), None),
            P(None, ("wide", "narrow")),
            P(("wide", "narrow"), None),
            P(("wide", "narrow")),
            P(("wide", "narrow"), None),
            P(None, ("wide", "narrow")),
            P(None, ("wide", "narrow"), None),
            P(None, ("wide", "narrow"), None),
            P(None, ("wide", "narrow")),
            P(("wide", "narrow"), None),
            P(("wide", "narrow")),
            P(("wide", "narrow"), None),
        ),
        check_vma=False,
    )
```

profile of v0, /device:TPU:0, one launch (start us, length us, event | category | flops | bytes accessed | tf_op | source)
XLA Modules:
  0.0 2429.0 jit_solution(2968353075150455257)
XLA Ops:
  12.0 70.8 %all_gather.57 = bf16[32,512]{0,1:T(8,128)(2,1)S(1)} all-gather(bf16[32,16]{0,1:T(8,128)(2,1)} %param.31), channel_id=1, replica_groups=mesh['wide'=16,'narrow'=2] {'wide','narrow'}, dimensions={1}, use_global_device_ids=true | all-gather | bytes 33792 | tf_op jit(solution)/shard_map/all_gather | solution.py:354
  83.7 64.2 %all-gather = bf16[32,16,7]{1,2,0:T(8,128)(2,1)S(1)} all-gather(bf16[1,16,7]{1,2,0:T(8,128)(2,1)} %bitcast.406), channel_id=1, replica_groups=mesh['wide'=16,'narrow'=2] {'wide','narrow'}, dimensions={0}, use_global_device_ids=true | all-gather | bytes 7392 | tf_op jit(solution)/shard_map/all_gather | solution.py:357
  148.3 65.2 %all-gather.2 = bf16[32,16,2]{1,2,0:T(2,128)(2,1)S(1)} all-gather(bf16[1,16,2]{1,2,0:T(2,128)(2,1)} %bitcast.419), channel_id=1, replica_groups=mesh['wide'=16,'narrow'=2] {'wide','narrow'}, dimensions={0}, use_global_device_ids=true | all-gather | bytes 2112 | tf_op jit(solution)/shard_map/all_gather | solution.py:345
  213.8 63.3 %all-gather.1 = bf16[32,16,2]{1,2,0:T(2,128)(2,1)S(1)} all-gather(bf16[1,16,2]{1,2,0:T(2,128)(2,1)} %bitcast.420), channel_id=1, replica_groups=mesh['wide'=16,'narrow'=2] {'wide','narrow'}, dimensions={0}, use_global_device_ids=true | all-gather | bytes 2112 | tf_op jit(solution)/shard_map/all_gather | solution.py:344
  277.3 67.4 %all_gather.60 = bf16[256,512]{0,1:T(8,128)(2,1)S(1)} all-gather(bf16[256,16]{0,1:T(8,128)(2,1)} %param.23), channel_id=1, replica_groups=mesh['wide'=16,'narrow'=2] {'wide','narrow'}, dimensions={1}, use_global_device_ids=true | all-gather | bytes 270336 | tf_op jit(solution)/shard_map/all_gather | solution.py:343
  344.8 64.1 %all-gather.3 = bf16[32,16,5]{1,2,0:T(8,128)(2,1)S(1)} all-gather(bf16[1,16,5]{1,2,0:T(8,128)(2,1)} %bitcast.407), channel_id=1, replica_groups=mesh['wide'=16,'narrow'=2] {'wide','narrow'}, dimensions={0}, use_global_device_ids=true | all-gather | bytes 5280 | tf_op jit(solution)/shard_map/all_gather | solution.py:347
  409.8 37.5 %all-reduce.7 = (bf16[1024]{0:T(1024)(128)(2,1)S(1)}, bf16[1024]{0:T(1024)(128)(2,1)S(1)}) all-reduce(bf16[1024]{0:T(1024)(128)(2,1)S(1)} %dynamic-update-slice, bf16[1024]{0:T(1024)(128)(2,1)S(1)} %dynamic-update-slice.1), channel_id=1, replica_groups=mesh['wide'=16,'narrow'=2] {'wide','narrow'}, use_global_device_ids=true, to_apply=%add.2 | all-reduce | flops 2048 | bytes 8192
  448.3 4.0 fusion.218
  452.3 7.7 fusion.125
  468.5 3.1 fusion.103
  482.8 4.6 multiply_reduce_fusion.1
  487.4 4.1 fusion.4
  491.6 3.4 copy-done.1
  495.0 10.0 fusion.90
  505.0 8.1 fusion.216
  513.5 11.0 multiply_convert_fusion.3
  524.5 3.5 fusion.217
  554.0 8.6 multiply_convert_fusion.4
  575.3 6.5 fusion.224
  581.8 3.2 fusion.94
  585.1 20.4 fusion.113
  605.4 20.2 fusion.91
  631.5 4.6 fusion.226
  636.1 6.4 fusion.104
  642.5 14.6 fusion.110
  657.1 14.2 fusion.107
  689.3 9.4 fusion.225
  698.7 12.3 fusion.97
  711.0 37.1 %fusion.84 = bf16[8,64,784]{2,1,0:T(8,128)(2,1)} fusion(bf16[784,8,64]{0,2,1:T(8,128)(2,1)S(1)} %bitcast.309, f32[8,784,784]{1,2,0:T(8,128)} %fusion.225, f32[8,784]{1,0:T(8,128)S(1)} %log_add_fusion, f32[8,784,784]{1,2,0:T(8,128)} %copy-done.1), kind=kOutput, calls=%fused_computation.118 | convolution fusion | flops 674071424 | bytes 40968704 | tf_op jit(solution)/shard_map/while/body/eval_jaxpr/hqk,khd->qhd/dot_general | solution.py:95
  748.1 31.2 %fusion.87 = bf16[8,64,784]{2,1,0:T(8,128)(2,1)S(1)} fusion(bf16[784,8,64]{0,2,1:T(8,128)(2,1)S(1)} %bitcast.307, f32[8,784,784]{1,2,0:T(8,128)} %fusion.225, f32[8,784]{1,0:T(8,128)S(1)} %log_add_fusion, f32[8,784,784]{1,2,0:T(8,128)} %copy-done.1), kind=kOutput, calls=%fused_computation.119 | convolution fusion | flops 674071424 | bytes 40968704 | tf_op jit(solution)/shard_map/while/body/eval_jaxpr/hqk,qhd->khd/dot_general | solution.py:99
  783.6 3.3 fusion.204
  804.7 3.4 fusion.142
  809.3 3.4 fusion.132
  813.3 4.6 fusion.194
  818.7 4.6 fusion.128
  847.0 42.9 %all-reduce.6 = (f32[1024]{0:T(1024)S(1)}, f32[1024]{0:T(1024)S(1)}) all-reduce(f32[1024]{0:T(1024)S(1)} %copy-done.95, f32[1024]{0:T(1024)S(1)} %copy-done.94), channel_id=7, replica_groups=mesh['wide'=16,'narrow'=2] {'wide','narrow'}, use_global_device_ids=true, to_apply=%region_39.40.clone | all-reduce | flops 2048 | bytes 16384
  893.4 30.3 %reduce-scatter.37.cloned.1.call-done = f32[16,2]{1,0:T(8,128)} async-done(((f32[512,2]{1,0:T(8,128)}), f32[16,2]{1,0:T(8,128)}) %reduce-scatter.37.cloned.1.call-update) | async-done | bytes 144
  925.0 130.8 %reduce-scatter.39.cloned.1.call-done = f32[16,5]{1,0:T(8,128)} async-done(((f32[512,5]{1,0:T(8,128)}), f32[16,5]{1,0:T(8,128)}) %reduce-scatter.39.cloned.1.call-update) | async-done | bytes 336
  1057.2 130.5 %reduce-scatter.41.cloned.1.call-done = f32[16,7]{1,0:T(8,128)} async-done(((f32[512,7]{1,0:T(8,128)}), f32[16,7]{1,0:T(8,128)}) %reduce-scatter.41.cloned.1.call-update) | async-done | bytes 464
  1189.0 131.3 %reduce-scatter.27.cloned.1.call-done = f32[32,16]{0,1:T(8,128)} async-done(((f32[32,512]{0,1:T(8,128)}), f32[32,16]{0,1:T(8,128)}) %reduce-scatter.27.cloned.1.call-update) | async-done | bytes 2064 | tf_op jit(solution)/shard_map/reduce_scatter | solution.py:389
  1320.3 132.5 %reduce-scatter.19.cloned.1.call-done = f32[256,16]{0,1:T(8,128)} async-done(((f32[256,512]{0,1:T(8,128)}), f32[256,16]{0,1:T(8,128)}) %reduce-scatter.19.cloned.1.call-update) | async-done | bytes 16400 | tf_op jit(solution)/shard_map/reduce_scatter | solution.py:429
  1452.9 136.5 %reduce-scatter.35.cloned.1.call-done = f32[32,512]{1,0:T(8,128)} async-done(((f32[1024,512]{1,0:T(8,128)}), f32[32,512]{1,0:T(8,128)}) %reduce-scatter.35.cloned.1.call-update) | async-done | bytes 65552 | tf_op jit(solution)/shard_map/reduce_scatter | solution.py:395
  1589.4 136.2 %reduce-scatter.33.cloned.1.call-done = f32[16,1024]{1,0:T(8,128)} async-done(((f32[512,1024]{1,0:T(8,128)}), f32[16,1024]{1,0:T(8,128)}) %reduce-scatter.33.cloned.1.call-update) | async-done | bytes 65552 | tf_op jit(solution)/shard_map/reduce_scatter | solution.py:393
  1725.6 136.5 %reduce-scatter.25.cloned.1.call-done = f32[32,512]{1,0:T(8,128)} async-done(((f32[1024,512]{1,0:T(8,128)}), f32[32,512]{1,0:T(8,128)}) %reduce-scatter.25.cloned.1.call-update) | async-done | bytes 65552 | tf_op jit(solution)/shard_map/reduce_scatter | solution.py:435
  1862.0 136.5 %reduce-scatter.23.cloned.1.call-done = f32[16,1024]{1,0:T(8,128)} async-done(((f32[512,1024]{1,0:T(8,128)}), f32[16,1024]{1,0:T(8,128)}) %reduce-scatter.23.cloned.1.call-update) | async-done | bytes 65552 | tf_op jit(solution)/shard_map/reduce_scatter | solution.py:433
  1998.5 140.8 %reduce-scatter.31.cloned.1.call-done = f32[4,16,512]{2,1,0:T(8,128)} async-done(((f32[4,512,512]{2,1,0:T(8,128)}), f32[4,16,512]{2,1,0:T(8,128)}) %reduce-scatter.31.cloned.1.call-update) | async-done | bytes 131088 | tf_op jit(solution)/shard_map/reduce_scatter | solution.py:391
  2139.3 141.8 %reduce-scatter.29.cloned.1.call-done = f32[4,16,512]{2,1,0:T(8,128)} async-done(((f32[4,512,512]{2,1,0:T(8,128)}), f32[4,16,512]{2,1,0:T(8,128)}) %reduce-scatter.29.cloned.1.call-update) | async-done | bytes 131088 | tf_op jit(solution)/shard_map/reduce_scatter | solution.py:390
  2281.1 141.2 %reduce-scatter.21.cloned.1.call-done = f32[4,16,512]{2,1,0:T(8,128)} async-done(((f32[4,512,512]{2,1,0:T(8,128)}), f32[4,16,512]{2,1,0:T(8,128)}) %reduce-scatter.21.cloned.1.call-update) | async-done | bytes 131088 | tf_op jit(solution)/shard_map/reduce_scatter | solution.py:431
  (414 shorter events, 144.9 us)
Async XLA Ops:
  7.2 445.1 %copy-start = (bf16[1,784,256]{2,1,0:T(8,128)(2,1)S(1)}, bf16[1,784,256]{2,1,0:T(8,128)(2,1)}, u32[]{:S(2)}) copy-start(bf16[1,784,256]{2,1,0:T(8,128)(2,1)} %param.19) | copy-start | bytes 1204228
  7.2 402.1 %copy-start.104 = (bf16[32]{0:T(256)(128)(2,1)S(1)}, bf16[32]{0:T(256)(128)(2,1)}, u32[]{:S(2)}) copy-start(bf16[32]{0:T(256)(128)(2,1)} %param.29) | copy-start | bytes 196
  7.2 402.3 %copy-start.105 = (bf16[32]{0:T(256)(128)(2,1)S(1)}, bf16[32]{0:T(256)(128)(2,1)}, u32[]{:S(2)}) copy-start(bf16[32]{0:T(256)(128)(2,1)} %param.36) | copy-start | bytes 196
  7.2 440.1 %copy-start.62 = (bf16[1,512,512]{2,1,0:T(8,128)(2,1)S(1)}, bf16[1,512,512]{2,1,0:T(8,128)(2,1)}, u32[]{:S(2)}) copy-start(bf16[1,512,512]{2,1,0:T(8,128)(2,1)} %param.22) | copy-start | bytes 1572868
  7.2 441.1 %copy-start.96 = (s32[1,512]{1,0:T(1,128)S(1)}, s32[1,512]{1,0:T(1,128)}, u32[]{:S(2)}) copy-start(s32[1,512]{1,0:T(1,128)} %param.20) | copy-start | bytes 6148
  7.2 452.7 %all-gather.12.cloned.1.call-start = ((), (), s32[]{:S(2)}) async-start(), calls=%async_computation.12 | async-start | bytes 2162688 | tf_op jit(solution)/shard_map/all_gather | solution.py:355
  8.0 464.5 %all-gather.14.cloned.1.call-start = ((), (), s32[]{:S(2)}) async-start(), calls=%async_computation.13 | async-start | bytes 2162688 | tf_op jit(solution)/shard_map/all_gather | solution.py:346
  8.7 504.8 %all-gather.16.cloned.1.call-start = ((), (), s32[]{:S(2)}) async-start(), calls=%async_computation.14 | async-start | bytes 1081344 | tf_op jit(solution)/shard_map/all_gather | solution.py:348
  9.5 515.1 %all-gather.18.cloned.1.call-start = ((), (), s32[]{:S(2)}) async-start(), calls=%async_computation.15 | async-start | bytes 1081344 | tf_op jit(solution)/shard_map/all_gather | solution.py:350
  10.0 519.7 %all-gather.20.cloned.1.call-start = ((), (), s32[]{:S(2)}) async-start(), calls=%async_computation.16 | async-start | bytes 2162688 | tf_op jit(solution)/shard_map/all_gather | solution.py:356
  10.6 543.3 %all-gather.22.cloned.1.call-start = ((), (), s32[]{:S(2)}) async-start(), calls=%async_computation.17 | async-start | bytes 1081344 | tf_op jit(solution)/shard_map/all_gather | solution.py:358
  11.2 551.3 %all-gather.24.cloned.1.call-start = ((), (), s32[]{:S(2)}) async-start(), calls=%async_computation.18 | async-start | bytes 1081344 | tf_op jit(solution)/shard_map/all_gather | solution.py:360
  11.9 911.8 %reduce-scatter.37.cloned.1.call-start = ((), (), s32[]{:S(2)}) async-start(), calls=%async_computation.28 | async-start | bytes 270336
  83.7 384.8 %copy-start.37 = (pred[512,512]{0,1:T(8,128)(4,1)}, pred[512,512]{0,1:T(8,128)(4,1)S(1)}, u32[]{:S(2)}) copy-start(pred[512,512]{0,1:T(8,128)(4,1)S(1)} %fusion.124) | copy-start | bytes 786436
  148.2 402.7 %copy-start.90 = (f32[1,512]{1,0:T(1,128)}, f32[1,512]{1,0:T(1,128)S(1)}, u32[]{:S(2)}) copy-start(f32[1,512]{1,0:T(1,128)S(1)} %get-tuple-element.478) | copy-start | bytes 6148
  148.2 414.3 %copy-start.91 = (f32[1,512]{1,0:T(1,128)}, f32[1,512]{1,0:T(1,128)S(1)}, u32[]{:S(2)}) copy-start(f32[1,512]{1,0:T(1,128)S(1)} %get-tuple-element.476) | copy-start | bytes 6148
  148.3 423.6 %copy-start.78 = (f32[1,512]{1,0:T(1,128)}, f32[1,512]{1,0:T(1,128)S(1)}, u32[]{:S(2)}) copy-start(f32[1,512]{1,0:T(1,128)S(1)} %get-tuple-element.477) | copy-start | bytes 6148
  148.3 480.4 %copy-start.68 = (f32[1,512]{1,0:T(1,128)}, f32[1,512]{1,0:T(1,128)S(1)}, u32[]{:S(2)}) copy-start(f32[1,512]{1,0:T(1,128)S(1)} %get-tuple-element.479) | copy-start | bytes 6148
  213.8 291.2 %copy-start.80 = (f32[1,512]{1,0:T(1,128)}, f32[1,512]{1,0:T(1,128)S(1)}, u32[]{:S(2)}) copy-start(f32[1,512]{1,0:T(1,128)S(1)} %get-tuple-element.485) | copy-start | bytes 6148
  277.3 182.6 %copy-start.82 = (f32[1,512]{1,0:T(1,128)}, f32[1,512]{1,0:T(1,128)S(1)}, u32[]{:S(2)}) copy-start(f32[1,512]{1,0:T(1,128)S(1)} %get-tuple-element.488) | copy-start | bytes 6148
  344.8 115.2 %copy-start.50 = (bf16[256,512]{0,1:T(8,128)(2,1)}, bf16[256,512]{0,1:T(8,128)(2,1)S(1)}, u32[]{:S(2)}) copy-start(bf16[256,512]{0,1:T(8,128)(2,1)S(1)} %all_gather.60) | copy-start | bytes 786436
  409.3 115.3 %copy-start.98 = (f32[1,512]{1,0:T(1,128)}, f32[1,512]{1,0:T(1,128)S(1)}, u32[]{:S(2)}) copy-start(f32[1,512]{1,0:T(1,128)S(1)} %get-tuple-element.483) | copy-start | bytes 6148
  409.3 274.0 %copy-start.92 = (f32[1,512]{1,0:T(1,128)}, f32[1,512]{1,0:T(1,128)S(1)}, u32[]{:S(2)}) copy-start(f32[1,512]{1,0:T(1,128)S(1)} %get-tuple-element.484) | copy-start | bytes 6148
  472.4 156.2 %copy-start.70 = (f32[512]{0:T(512)}, f32[512]{0:T(512)S(1)}, u32[]{:S(2)}) copy-start(f32[512]{0:T(512)S(1)} %fusion.160) | copy-start | bytes 6148
  513.5 169.8 %copy-start.88 = (f32[784]{0:T(1024)}, f32[784]{0:T(1024)S(1)}, u32[]{:S(2)}) copy-start(f32[784]{0:T(1024)S(1)} %fusion.146) | copy-start | bytes 9412
  552.8 19.1 copy-start.71
  572.3 53.4 %copy-start.72 = (f32[512]{0:T(512)}, f32[512]{0:T(512)S(1)}, u32[]{:S(2)}) copy-start(f32[512]{0:T(512)S(1)} %negate_multiply_fusion.5) | copy-start | bytes 6148
  605.4 20.2 copy-start.65
  605.4 20.2 copy-start.67
  676.6 111.3 %copy-start.86 = (f32[784]{0:T(1024)}, f32[784]{0:T(1024)S(1)}, u32[]{:S(2)}) copy-start(f32[784]{0:T(1024)S(1)} %negate_multiply_fusion.3) | copy-start | bytes 9412
  684.0 99.6 %copy-start.84 = (f32[784]{0:T(1024)}, f32[784]{0:T(1024)S(1)}, u32[]{:S(2)}) copy-start(f32[784]{0:T(1024)S(1)} %negate_multiply_fusion.2) | copy-start | bytes 9412
  711.0 37.1 %copy-start.17 = (bf16[784,512]{0,1:T(8,128)(2,1)S(1)}, bf16[784,512]{0,1:T(8,128)(2,1)}, u32[]{:S(2)}) copy-start(bf16[784,512]{0,1:T(8,128)(2,1)} %copy-done.16) | copy-start | bytes 2408452
  787.8 268.0 %reduce-scatter.39.cloned.1.call-start = ((), (), s32[]{:S(2)}) async-start(), calls=%async_computation.29 | async-start | bytes 270336
  791.8 395.9 %reduce-scatter.41.cloned.1.call-start = ((), (), s32[]{:S(2)}) async-start(), calls=%async_computation.30 | async-start | bytes 270336
  796.3 524.1 %reduce-scatter.27.cloned.1.call-start = ((), (), s32[]{:S(2)}) async-start(), calls=%async_computation.23 | async-start | bytes 270336 | tf_op jit(solution)/shard_map/reduce_scatter | solution.py:389
  801.9 651.0 %reduce-scatter.19.cloned.1.call-start = ((), (), s32[]{:S(2)}) async-start(), calls=%async_computation.19 | async-start | bytes 540672 | tf_op jit(solution)/shard_map/reduce_scatter | solution.py:429
  804.7 784.7 %reduce-scatter.35.cloned.1.call-start = ((), (), s32[]{:S(2)}) async-start(), calls=%async_computation.27 | async-start | bytes 2162688 | tf_op jit(solution)/shard_map/reduce_scatter | solution.py:395
  808.1 917.5 %reduce-scatter.33.cloned.1.call-start = ((), (), s32[]{:S(2)}) async-start(), calls=%async_computation.26 | async-start | bytes 2162688 | tf_op jit(solution)/shard_map/reduce_scatter | solution.py:393
  812.7 1049.4 %reduce-scatter.25.cloned.1.call-start = ((), (), s32[]{:S(2)}) async-start(), calls=%async_computation.22 | async-start | bytes 2162688 | tf_op jit(solution)/shard_map/reduce_scatter | solution.py:435
  818.0 1180.5 %reduce-scatter.23.cloned.1.call-start = ((), (), s32[]{:S(2)}) async-start(), calls=%async_computation.21 | async-start | bytes 2162688 | tf_op jit(solution)/shard_map/reduce_scatter | solution.py:433
  823.3 1315.9 %reduce-scatter.31.cloned.1.call-start = ((), (), s32[]{:S(2)}) async-start(), calls=%async_computation.25 | async-start | bytes 4325376 | tf_op jit(solution)/shard_map/reduce_scatter | solution.py:391
  831.9 1449.2 %reduce-scatter.29.cloned.1.call-start = ((), (), s32[]{:S(2)}) async-start(), calls=%async_computation.24 | async-start | bytes 4325376 | tf_op jit(solution)/shard_map/reduce_scatter | solution.py:390
  838.1 1584.2 %reduce-scatter.21.cloned.1.call-start = ((), (), s32[]{:S(2)}) async-start(), calls=%async_computation.20 | async-start | bytes 4325376 | tf_op jit(solution)/shard_map/reduce_scatter | solution.py:431
  846.3 44.8 %copy-start.40 = (bf16[1,512,512]{1,2,0:T(8,128)(2,1)S(1)}, bf16[1,512,512]{1,2,0:T(8,128)(2,1)}, u32[]{:S(2)}) copy-start(bf16[1,512,512]{1,2,0:T(8,128)(2,1)} %get-tuple-element.442) | copy-start | bytes 1572868
  846.3 45.8 %copy-start.8 = (f32[784,512]{1,0:T(8,128)S(1)}, f32[784,512]{1,0:T(8,128)}, u32[]{:S(2)}) copy-start(f32[784,512]{1,0:T(8,128)} %get-tuple-element.514) | copy-start | bytes 4816900
  846.3 45.8 %copy-start.51 = (bf16[256,512]{0,1:T(8,128)(2,1)S(1)}, bf16[256,512]{0,1:T(8,128)(2,1)}, u32[]{:S(2)}) copy-start(bf16[256,512]{0,1:T(8,128)(2,1)} %copy-done.50) | copy-start | bytes 786436
  846.3 45.8 %copy-start.81 = (f32[1,512]{1,0:T(1,128)S(1)}, f32[1,512]{1,0:T(1,128)}, u32[]{:S(2)}) copy-start(f32[1,512]{1,0:T(1,128)} %copy-done.80) | copy-start | bytes 6148
  846.3 45.8 %copy-start.83 = (f32[1,512]{1,0:T(1,128)S(1)}, f32[1,512]{1,0:T(1,128)}, u32[]{:S(2)}) copy-start(f32[1,512]{1,0:T(1,128)} %copy-done.82) | copy-start | bytes 6148
  (89 other events, 326.2 us)
Sparse Core Ops, SparseCore 0:
  11.1 59.1 all-gather.11
  73.4 55.1 all-gather.13
  131.5 52.7 all-gather.15
  187.0 52.6 all-gather.17
  242.6 55.5 all-gather.19
  300.9 52.6 all-gather.21
  356.5 52.8 all-gather.23
  787.9 135.7 reduce-scatter.36
  926.0 129.7 reduce-scatter.38
  1057.9 129.7 reduce-scatter.40
  1190.6 129.7 reduce-scatter.26
  1323.0 129.8 reduce-scatter.18
  1455.8 133.5 reduce-scatter.34
  1592.1 133.4 reduce-scatter.32
  1728.4 133.6 reduce-scatter.24
  1864.7 133.7 reduce-scatter.22
  2001.3 137.9 reduce-scatter.30
  2142.1 138.9 reduce-scatter.28
  2284.0 138.1 reduce-scatter.20
where the time goes:
time: 2430 us
  waiting for transfers between devices  1530 us (63%)
  blocking collectives  476 us (20%)
  matrix products  334 us (14%)
  local copies, waits for them, and re-layouts  47.4 us (2%)
  other arithmetic  25.6 us (1%)
    unnamed x22, waiting for transfers between devices  296 us
    reduce_scatter x1, waiting for transfers between devices, body(): lax.psum_scatter(decoder_totals[1], ('wide', 'narrow'), scatter_dimension...  142 us
    reduce_scatter x1, waiting for transfers between devices, body(): lax.psum_scatter(encoder_totals[2], ('wide', 'narrow'), scatter_dimension...  141 us
    reduce_scatter x1, waiting for transfers between devices, body(): lax.psum_scatter(decoder_totals[2], ('wide', 'narrow'), scatter_dimension...  141 us
    reduce_scatter x1, waiting for transfers between devices, body(): lax.psum_scatter(decoder_totals[6], ('wide', 'narrow'), scatter_dimension...  137 us
    reduce_scatter x1, waiting for transfers between devices, body(): lax.psum_scatter(encoder_totals[4], ('wide', 'narrow'), scatter_dimension...  136 us
    reduce_scatter x1, waiting for transfers between devices, body(): lax.psum_scatter(encoder_totals[6], ('wide', 'narrow'), scatter_dimension...  136 us
    reduce_scatter x1, waiting for transfers between devices, body(): lax.psum_scatter(decoder_totals[4], ('wide', 'narrow'), scatter_dimension...  136 us
  transfers between devices with their start and end apart: 19, of which 12 were waited for; matrix products, arithmetic and copies ran while one was open for 7% of the time, Pallas kernels for 0%

commit v1 on v0

--- a/solution.py
+++ b/solution.py
@@ -314,15 +314,10 @@
     )
 
 
-def zeros_like_all(shapes_from):
-    return jax.tree.map(lambda item: jnp.zeros(item.shape, jnp.float32), shapes_from)
-
-
-def body(
-    features,
-    tag_ids,
-    tag_lengths,
-    out_cot,
+AXES = ("wide", "narrow")
+
+
+def pack_parameters(
     proj_weight,
     bn_given,
     bn_affine,
@@ -339,118 +334,174 @@
     dec_hidden_bias,
     dec_ffn_out,
 ):
-    encoder_full = (
-        lax.all_gather(proj_weight, ("wide", "narrow"), axis=1, tiled=True),
-        lax.all_gather(bn_given, ("wide", "narrow"), axis=1, tiled=True),
-        lax.all_gather(bn_affine, ("wide", "narrow"), axis=1, tiled=True),
-        lax.all_gather(enc_attn, ("wide", "narrow"), axis=1, tiled=True),
-        lax.all_gather(enc_vec, ("wide", "narrow"), axis=1, tiled=True),
-        lax.all_gather(enc_ffn_in, ("wide", "narrow"), axis=0, tiled=True),
-        lax.all_gather(enc_hidden_bias, ("wide", "narrow"), axis=0, tiled=True),
-        lax.all_gather(enc_ffn_out, ("wide", "narrow"), axis=0, tiled=True),
-    )
-    memories, encoder_stored = lax.map(partial(encoder_forward, encoder_full), features)
-    decoder_full = (
-        lax.all_gather(tag_table, ("wide", "narrow"), axis=1, tiled=True),
-        lax.all_gather(dec_self, ("wide", "narrow"), axis=1, tiled=True),
-        lax.all_gather(dec_cross, ("wide", "narrow"), axis=1, tiled=True),
-        lax.all_gather(dec_vec, ("wide", "narrow"), axis=1, tiled=True),
-        lax.all_gather(dec_ffn_in, ("wide", "narrow"), axis=0, tiled=True),
-        lax.all_gather(dec_hidden_bias, ("wide", "narrow"), axis=0, tiled=True),
-        lax.all_gather(dec_ffn_out, ("wide", "narrow"), axis=0, tiled=True),
-    )
-
-    def decode_one(table_item):
-        return decoder_forward(decoder_full, table_item[0], table_item[1], table_item[2])
-
-    decoded_full, decoder_stored = lax.map(decode_one, (memories, tag_ids, tag_lengths))
-    decoder_back = (
-        lax.all_gather(tag_table, ("wide", "narrow"), axis=1, tiled=True),
-        lax.all_gather(dec_self, ("wide", "narrow"), axis=1, tiled=True),
-        lax.all_gather(dec_cross, ("wide", "narrow"), axis=1, tiled=True),
-        lax.all_gather(dec_vec, ("wide", "narrow"), axis=1, tiled=True),
-        lax.all_gather(dec_ffn_in, ("wide", "narrow"), axis=0, tiled=True),
-        lax.all_gather(dec_hidden_bias, ("wide", "narrow"), axis=0, tiled=True),
-        lax.all_gather(dec_ffn_out, ("wide", "narrow"), axis=0, tiled=True),
-    )
-
-    def decoder_step(totals, table_item):
-        grads, grad_memory = decoder_backward(
-            decoder_back, table_item[0], table_item[1], table_item[2], table_item[3], table_item[4]
+    rows = proj_weight.shape[1]
+    width = enc_attn.shape[2]
+    columns = jnp.concatenate(
+        [
+            proj_weight,
+            bn_given,
+            bn_affine,
+            enc_vec,
+            dec_vec,
+            tag_table,
+            enc_hidden_bias.reshape(rows, -1).T,
+            dec_hidden_bias.reshape(rows, -1).T,
+        ],
+        axis=0,
+    )
+    columns = jnp.pad(columns, ((0, width - columns.shape[0]), (0, 0))).T
+    return jnp.concatenate(
+        [
+            columns,
+            enc_attn.reshape(4 * rows, width),
+            enc_ffn_in[:, :width],
+            enc_ffn_in[:, width:],
+            enc_ffn_out,
+            dec_self.reshape(4 * rows, width),
+            dec_cross.reshape(4 * rows, width),
+            dec_ffn_in[:, :width],
+            dec_ffn_in[:, width:],
+            dec_ffn_out,
+        ],
+        axis=0,
+    )
+
+
+def unpack_parameters(gathered, rows, channels, vocab):
+    count, width = gathered.shape[0], gathered.shape[2]
+    total = count * rows
+
+    def stack(start, pieces):
+        part = gathered[:, start * rows : (start + pieces) * rows]
+        return part.reshape(count, pieces, rows, width).swapaxes(0, 1).reshape(pieces, total, width)
+
+    def tall(start):
+        return gathered[:, start * rows : (start + 2) * rows].reshape(2 * total, width)
+
+    columns = stack(0, 1)[0].T
+    sizes = (channels, 2, 2, 5, 7, vocab, 2, 2)
+    parts, at = [], 0
+    for size in sizes:
+        parts.append(columns[at : at + size])
+        at += size
+    proj_weight, bn_given, bn_affine, enc_vec, dec_vec, tag_table, enc_hidden, dec_hidden = parts
+    enc_in, dec_in = stack(5, 2), stack(17, 2)
+    encoder = (
+        proj_weight,
+        bn_given,
+        bn_affine,
+        stack(1, 4),
+        enc_vec,
+        jnp.concatenate([enc_in[0], enc_in[1]], axis=1),
+        enc_hidden.T.reshape(-1),
+        tall(7),
+    )
+    decoder = (
+        tag_table,
+        stack(9, 4),
+        stack(13, 4),
+        dec_vec,
+        jnp.concatenate([dec_in[0], dec_in[1]], axis=1),
+        dec_hidden.T.reshape(-1),
+        tall(19),
+    )
+    return encoder, decoder
+
+
+def pack_gradients(encoder, decoder, count):
+    proj_weight, bn_affine, enc_attn, enc_vec, enc_in, enc_hidden, enc_out = encoder
+    tag_table, dec_self, dec_cross, dec_vec, dec_in, dec_hidden, dec_out = decoder
+    width = enc_attn.shape[2]
+    columns = jnp.concatenate(
+        [
+            proj_weight,
+            bn_affine,
+            enc_vec,
+            dec_vec,
+            tag_table,
+            enc_hidden.reshape(width, -1).T,
+            dec_hidden.reshape(width, -1).T,
+        ],
+        axis=0,
+    )
+    columns = jnp.pad(columns, ((0, width - columns.shape[0]), (0, 0))).T
+
+    def spread(stack):
+        pieces, total, _ = stack.shape
+        return stack.reshape(pieces, count, total // count, width).swapaxes(0, 1).reshape(
+            count, -1, width
         )
-        return (jax.tree.map(jnp.add, totals, grads), grad_memory)
-
-    decoder_totals, grad_memories = lax.scan(
-        decoder_step,
-        zeros_like_all(decoder_back),
-        (memories, tag_ids, tag_lengths, out_cot, decoder_stored),
-    )
-    decoder_shares = (
-        lax.psum_scatter(decoder_totals[0], ("wide", "narrow"), scatter_dimension=1, tiled=True),
-        lax.psum_scatter(decoder_totals[1], ("wide", "narrow"), scatter_dimension=1, tiled=True),
-        lax.psum_scatter(decoder_totals[2], ("wide", "narrow"), scatter_dimension=1, tiled=True),
-        lax.psum_scatter(decoder_totals[3], ("wide", "narrow"), scatter_dimension=1, tiled=True),
-        lax.psum_scatter(decoder_totals[4], ("wide", "narrow"), scatter_dimension=0, tiled=True),
-        lax.psum_scatter(decoder_totals[5], ("wide", "narrow"), scatter_dimension=0, tiled=True),
-        lax.psum_scatter(decoder_totals[6], ("wide", "narrow"), scatter_dimension=0, tiled=True),
-    )
-    encoder_back = (
-        lax.all_gather(proj_weight, ("wide", "narrow"), axis=1, tiled=True),
-        lax.all_gather(bn_given, ("wide", "narrow"), axis=1, tiled=True),
-        lax.all_gather(bn_affine, ("wide", "narrow"), axis=1, tiled=True),
-        lax.all_gather(enc_attn, ("wide", "narrow"), axis=1, tiled=True),
-        lax.all_gather(enc_vec, ("wide", "narrow"), axis=1, tiled=True),
-        lax.all_gather(enc_ffn_in, ("wide", "narrow"), axis=0, tiled=True),
-        lax.all_gather(enc_hidden_bias, ("wide", "narrow"), axis=0, tiled=True),
-        lax.all_gather(enc_ffn_out, ("wide", "narrow"), axis=0, tiled=True),
-    )
-
-    def encoder_step(totals, table_item):
-        grads, grad_features = encoder_backward(
-            encoder_back, table_item[0], table_item[1], table_item[2]
-        )
-        return (jax.tree.map(jnp.add, totals, grads), grad_features)
-
-    encoder_zeros = zeros_like_all(
-        (
-            encoder_back[0],
-            encoder_back[2],
-            encoder_back[3],
-            encoder_back[4],
-            encoder_back[5],
-            encoder_back[6],
-            encoder_back[7],
-        )
-    )
-    encoder_totals, grad_features = lax.scan(
-        encoder_step, encoder_zeros, (features, grad_memories, encoder_stored)
-    )
-    encoder_shares = (
-        lax.psum_scatter(encoder_totals[0], ("wide", "narrow"), scatter_dimension=1, tiled=True),
-        lax.psum_scatter(encoder_totals[1], ("wide", "narrow"), scatter_dimension=1, tiled=True),
-        lax.psum_scatter(encoder_totals[2], ("wide", "narrow"), scatter_dimension=1, tiled=True),
-        lax.psum_scatter(encoder_totals[3], ("wide", "narrow"), scatter_dimension=1, tiled=True),
-        lax.psum_scatter(encoder_totals[4], ("wide", "narrow"), scatter_dimension=0, tiled=True),
-        lax.psum_scatter(encoder_totals[5], ("wide", "narrow"), scatter_dimension=0, tiled=True),
-        lax.psum_scatter(encoder_totals[6], ("wide", "narrow"), scatter_dimension=0, tiled=True),
-    )
+
+    def halves(matrix):
+        return jnp.stack([matrix[:, :width], matrix[:, width:]])
+
+    return jnp.concatenate(
+        [
+            spread(columns[None]),
+            spread(enc_attn),
+            spread(halves(enc_in)),
+            enc_out.reshape(count, -1, width),
+            spread(dec_self),
+            spread(dec_cross),
+            spread(halves(dec_in)),
+            dec_out.reshape(count, -1, width),
+        ],
+        axis=1,
+    ).astype(jnp.bfloat16)
+
+
+def unpack_gradients(share, rows, channels, vocab):
+    share = share.astype(jnp.float32)
+    width = share.shape[1]
+
+    def stack(start, pieces):
+        return share[start * rows : (start + pieces) * rows].reshape(pieces, rows, width)
+
+    columns = share[:rows].T
+    sizes = (channels, 2, 5, 7, vocab, 2, 2)
+    parts, at = [], 0
+    for size in sizes:
+        parts.append(columns[at : at + size])
+        at += size
+    proj_weight, bn_affine, enc_vec, dec_vec, tag_table, enc_hidden, dec_hidden = parts
+    enc_in, dec_in = stack(5, 2), stack(17, 2)
     return (
-        decoded_full.astype(jnp.bfloat16),
-        grad_features,
-        encoder_shares[0],
-        encoder_shares[1],
-        encoder_shares[2],
-        encoder_shares[3],
-        encoder_shares[4],
-        encoder_shares[5],
-        encoder_shares[6],
-        decoder_shares[0],
-        decoder_shares[1],
-        decoder_shares[2],
-        decoder_shares[3],
-        decoder_shares[4],
-        decoder_shares[5],
-        decoder_shares[6],
+        proj_weight,
+        bn_affine,
+        stack(1, 4),
+        enc_vec,
+        jnp.concatenate([enc_in[0], enc_in[1]], axis=1),
+        enc_hidden.T.reshape(-1),
+        share[7 * rows : 9 * rows],
+        tag_table,
+        stack(9, 4),
+        stack(13, 4),
+        dec_vec,
+        jnp.concatenate([dec_in[0], dec_in[1]], axis=1),
+        dec_hidden.T.reshape(-1),
+        share[19 * rows : 21 * rows],
+    )
+
+
+def body(features, tag_ids, tag_lengths, out_cot, *parameters):
+    rows, channels = parameters[0].shape[1], parameters[0].shape[0]
+    vocab = parameters[8].shape[0]
+    gathered = lax.all_gather(pack_parameters(*parameters), AXES, axis=0)
+    encoder_full, decoder_full = unpack_parameters(gathered, rows, channels, vocab)
+    memory, encoder_stored = encoder_forward(encoder_full, features[0])
+    decoded, decoder_stored = decoder_forward(decoder_full, memory, tag_ids[0], tag_lengths[0])
+    decoder_grads, grad_memory = decoder_backward(
+        decoder_full, memory, tag_ids[0], tag_lengths[0], out_cot[0], decoder_stored
+    )
+    encoder_grads, grad_features = encoder_backward(
+        encoder_full, features[0], grad_memory, encoder_stored
+    )
+    packed = pack_gradients(encoder_grads, decoder_grads, gathered.shape[0])
+    share = lax.psum_scatter(packed, AXES, scatter_dimension=0, tiled=False)
+    return (
+        decoded.astype(jnp.bfloat16)[None],
+        grad_features[None],
+        *unpack_gradients(share, rows, channels, vocab),
     )
 
 

time: 2430 us -> 701 us (0.29)
  waiting for transfers between devices: 1530 us -> 227 us
  blocking collectives: 476 us -> 0 us
  local copies, waits for them, and re-layouts: 47.4 us -> 102 us
  matrix products: 334 us -> 302 us
    reduce_scatter x9 -> x1, waiting for transfers between devices: 1230 us -> 139 us  [body(): share = lax.psum_scatter(packed, AXES, scatter_dimension=0, tiled=False)]
    all_gather x6 -> x0, blocking collectives: 395 us -> none  [the longest x1 70.8 us: body(): lax.all_gather(tag_table, ('wide', 'narrow'), axis=1, tiled=True)]
    unnamed x22 -> x2, waiting for transfers between devices: 296 us -> 0.03 us
    all_gather x7 -> x1, waiting for transfers between devices: 0.08 us -> 88.3 us  [body(): gathered = lax.all_gather(pack_parameters(*parameters), AXES, axis=0)]
    unnamed x2 -> x0, blocking collectives: 80.4 us -> none
  transfers between devices with their start and end apart: 19 -> 2, of which waited for: 12 -> 2; matrix products, arithmetic and copies ran while one was open for 7% -> 1% of each run, Pallas kernels for 0% -> 0%
where the time goes in v1:
time: 701 us; the launch traced here: 692 us
  matrix products  302 us (43%)
  waiting for transfers between devices  227 us (32%)
  local copies, waits for them, and re-layouts  102 us (15%)
  other arithmetic  42.9 us (6%)
  between operations  17.2 us (2%)
    reduce_scatter x1, waiting for transfers between devices, body(): share = lax.psum_scatter(packed, AXES, scatter_dimension=0, tiled=False)  139 us
    all_gather x1, waiting for transfers between devices, body(): gathered = lax.all_gather(pack_parameters(*parameters), AXES, axis=0)  88.3 us
    dot_general x3, matrix products, attend_backward(): jnp.einsum('hqk,qhd->khd', grad_raw, split_heads(query_rows), preferred_e...  66.3 us
    dot_general x3, matrix products, attend_backward(): jnp.einsum('hqk,khd->qhd', grad_raw, split_heads(key_rows), preferred_ele...  65.8 us
    dot_general x17, matrix products, product(): return jnp.dot(left, right, preferred_element_type=jnp.float32)  54.9 us
    unnamed x407, local copies, waits for them, and re-layouts  39.5 us
    dot_general x17, matrix products, product_outer(): lax.dot_general(left, right, (((1,), (1,)), ((), ())), preferred_element_...  23.7 us
    dot_general x17, matrix products, product_inner(): lax.dot_general(left, right, (((0,), (0,)), ((), ())), preferred_element_...  23.1 us
  transfers between devices with their start and end apart: 2, of which 2 were waited for; matrix products, arithmetic and copies ran while one was open for 1% of the time, Pallas kernels for 0%

profile of v1, /device:TPU:0, one launch (start us, length us, event | category | flops | bytes accessed | tf_op | source)
XLA Modules:
  0.0 692.0 jit_solution(6018228486203069162)
XLA Ops:
  23.8 88.3 %all-gather.3.cloned.1.call-done = bf16[10752,512]{1,0:T(8,128)(2,1)} async-done(((bf16[336,512]{1,0:T(8,128)(2,1)}), bf16[10752,512]{1,0:T(8,128)(2,1)}) %all-gather.3.cloned.1.call-update) | async-done | bytes 11010064 | tf_op jit(solution)/shard_map/all_gather | solution.py:489
  114.6 5.2 fusion.260
  119.8 2.5 fusion.261
  128.5 3.1 fusion.262
  134.1 5.0 fusion.164
  145.9 7.8 %fusion.157 = (bf16[784,512]{1,0:T(8,128)(2,1)S(1)}, f32[512,784]{0,1:T(8,128)}) fusion(f32[512]{0:T(512)S(1)} %fusion.199, f32[512]{0:T(512)S(1)} %get-tuple-element.94, f32[512]{0:T(512)S(1)} %get-tuple-element.93, pred[512]{0:T(512)(128)(4,1)S(1)} %fusion.193, f32[512]{0:T(512)S(1)} %get-tuple-element.194, f32[512]{0:T(512)S(1)} %get-tuple-element.195, ...), kind=kOutput, calls=%fused_computation.235 | convolution fusion | flops 208732160 | bytes 3082752 | tf_op jit(solution)/shard_map/dot_general | solution.py:13
  155.9 3.0 convolution_convert_fusion.8
  161.9 2.5 copy.140
  169.2 2.5 fusion.115
  171.8 5.8 fusion.254
  177.8 3.1 multiply_reduce_fusion.1
  181.0 4.1 fusion.4
  185.1 3.3 copy-done.1
  189.1 10.0 %fusion.102 = bf16[8,64,784]{2,1,0:T(8,128)(2,1)S(1)} fusion(bf16[784,8,64]{0,2,1:T(8,128)(2,1)S(1)} %bitcast.409, f32[8,784,784]{1,2,0:T(8,128)} %copy-done.1, f32[8,784]{1,0:T(8,128)S(1)} %fusion.4, f32[8,784]{1,0:T(8,128)S(1)} %get-tuple-element.168), kind=kOutput, calls=%fused_computation.138 | convolution fusion | flops 649478144 | bytes 21324800 | tf_op jit(solution)/shard_map/hqk,khd->qhd/dot_general | solution.py:70
  199.3 8.0 %fusion.258 = (f32[784]{0:T(1024)S(1)}, f32[784,512]{1,0:T(8,128)S(1)}, f32[784,512]{1,0:T(8,128)}) fusion(f32[512]{0:T(512)S(1)} %fusion.199, pred[512]{0:T(512)(128)(4,1)S(1)} %copy-done.159, f32[512]{0:T(512)S(1)} %copy-done.140, f32[512]{0:T(512)S(1)} %copy-done.115, f32[512,784]{0,1:T(8,128)S(1)} %copy-done.16, bf16[784,512]{0,1:T(8,128)(2,1)S(1)} %bitcast.526, ...), kind=kOutput, calls=%fused_computation.404 | convolution fusion | flops 413850880 | bytes 6153792 | tf_op jit(solution)/shard_map/dot_general | solution.py:13
  207.7 9.5 %multiply_convert_fusion.3 = (bf16[784,1024]{1,0:T(8,128)(2,1)S(1)}, f32[784,1024]{1,0:T(8,128)}, f32[784,1024]{1,0:T(8,128)}) fusion(f32[1024]{0:T(1024)S(1)} %copy-done.161, bf16[512,512]{1,0:T(8,128)(2,1)S(1)} %bitcast.504, bf16[512,512]{1,0:T(8,128)(2,1)S(1)} %bitcast.502, f32[784,512]{1,0:T(8,128)S(1)} %get-tuple-element.116, f32[512]{0:T(512)S(1)} %copy-done.137, ...), kind=kOutput, calls=%fused_computation.61 | convolution fusion | flops 879173632 | bytes 10696832 | tf_op jit(solution)/shard_map/dot_general | solution.py:13
  217.3 2.4 fusion.256
  221.7 2.2 copy.144
  223.9 2.6 convolution_convert_fusion.6
  231.7 2.1 fusion.8
  233.9 3.2 fusion.128
  238.5 5.1 multiply_convert_fusion.4
  256.5 6.5 fusion.274
  263.1 2.5 fusion.106
  265.5 20.1 %fusion.125 = bf16[8,64,512]{2,1,0:T(8,128)(2,1)} fusion(bf16[784,8,64]{0,2,1:T(8,128)(2,1)} %bitcast.441, f32[8,512,784]{1,2,0:T(8,128)} %fusion.274, f32[8,512,784]{1,2,0:T(8,128)} %copy-done.2, f32[8,512]{1,0:T(8,128)S(1)} %log_add_fusion.2), kind=kOutput, calls=%fused_computation.176 | convolution fusion | flops 440210176 | bytes 27033600 | tf_op jit(solution)/shard_map/hqk,khd->qhd/dot_general | solution.py:95
  285.6 20.3 %fusion.103 = bf16[8,64,784]{2,1,0:T(8,128)(2,1)} fusion(bf16[512,8,64]{0,2,1:T(8,128)(2,1)} %bitcast.501, f32[8,512,784]{1,2,0:T(8,128)} %fusion.274, f32[8,512,784]{1,2,0:T(8,128)} %copy-done.2, f32[8,512]{1,0:T(8,128)S(1)} %log_add_fusion.2), kind=kOutput, calls=%fused_computation.139 | convolution fusion | flops 440349440 | bytes 27033600 | tf_op jit(solution)/shard_map/hqk,qhd->khd/dot_general | solution.py:99
  305.9 2.2 fusion.275
  311.4 2.4 convolution_convert_fusion
  314.9 2.9 fusion.272
  317.9 3.3 multiply_reduce_fusion.6
  321.2 2.5 convolution_convert_fusion.1
  326.8 4.6 fusion.279
  331.4 3.1 fusion.116
  334.5 14.4 %fusion.119 = bf16[8,64,512]{2,1,0:T(8,128)(2,1)} fusion(bf16[512,8,64]{0,2,1:T(8,128)(2,1)} %bitcast.449, f32[8,512,512]{1,2,0:T(8,128)} %fusion.279, f32[8,512,512]{1,2,0:T(8,128)} %copy-done.3, f32[8,512]{1,0:T(8,128)S(1)} %copy-done.132, pred[512,512]{0,1:T(8,128)(4,1)S(1)} %copy-done.43), kind=kOutput, calls=%fused_computation.174 | convolution fusion | flops 291770880 | bytes 18104320 | tf_op jit(solution)/shard_map/hqk,khd->qhd/dot_general | solution.py:95
  349.0 14.4 %fusion.122 = bf16[8,64,512]{2,1,0:T(8,128)(2,1)} fusion(bf16[512,8,64]{0,2,1:T(8,128)(2,1)S(1)} %bitcast.448, f32[8,512,512]{1,2,0:T(8,128)} %fusion.279, f32[8,512,512]{1,2,0:T(8,128)} %copy-done.3, f32[8,512]{1,0:T(8,128)S(1)} %copy-done.132, pred[512,512]{0,1:T(8,128)(4,1)S(1)} %copy-done.43), kind=kOutput, calls=%fused_computation.175 | convolution fusion | flops 291770880 | bytes 18104320 | tf_op jit(solution)/shard_map/hqk,qhd->khd/dot_general | solution.py:99
  363.4 2.6 fusion.249
  370.7 11.7 %fusion.276 = f32[8,784,784]{1,2,0:T(8,128)} fusion(bf16[784,8,64]{0,2,1:T(8,128)(2,1)S(1)} %bitcast.395, bf16[784,8,64]{0,2,1:T(8,128)(2,1)} %bitcast.410), kind=kOutput, calls=%fused_computation.421 | convolution fusion | flops 629407744 | bytes 21274624 | tf_op jit(solution)/shard_map/qhd,khd->hqk/dot_general | solution.py:90
  382.4 12.2 %fusion.109 = bf16[8,64,784]{2,1,0:T(8,128)(2,1)} fusion(bf16[784,8,64]{0,2,1:T(8,128)(2,1)S(1)} %bitcast.396, f32[8,784]{1,0:T(8,128)S(1)} %copy-done.94, f32[8,784,784]{1,2,0:T(8,128)} %copy-done.1), kind=kOutput, calls=%fused_computation.141 | convolution fusion | flops 644560896 | bytes 21299712 | tf_op jit(solution)/shard_map/hqk,qhd->khd/dot_general | solution.py:86
  394.6 31.3 %fusion.96 = bf16[8,64,784]{2,1,0:T(8,128)(2,1)} fusion(bf16[784,8,64]{0,2,1:T(8,128)(2,1)} %bitcast.412, f32[8,784,784]{1,2,0:T(8,128)} %fusion.276, f32[8,784]{1,0:T(8,128)S(1)} %copy-done.94, f32[8,784,784]{1,2,0:T(8,128)} %copy-done.1), kind=kOutput, calls=%fused_computation.136 | convolution fusion | flops 674071424 | bytes 40968704 | tf_op jit(solution)/shard_map/hqk,khd->qhd/dot_general | solution.py:95
  426.0 31.6 %fusion.99 = bf16[8,64,784]{2,1,0:T(8,128)(2,1)} fusion(bf16[784,8,64]{0,2,1:T(8,128)(2,1)S(1)} %bitcast.414, f32[8,784,784]{1,2,0:T(8,128)} %fusion.276, f32[8,784]{1,0:T(8,128)S(1)} %copy-done.94, f32[8,784,784]{1,2,0:T(8,128)} %copy-done.1), kind=kOutput, calls=%fused_computation.137 | convolution fusion | flops 674071424 | bytes 40968704 | tf_op jit(solution)/shard_map/hqk,qhd->khd/dot_general | solution.py:99
  457.7 7.8 %fusion.153 = (bf16[512,512]{1,0:T(8,128)(2,1)}, bf16[512,512]{1,0:T(8,128)(2,1)S(1)}) fusion(f32[512,512]{0,1:T(8,128)} %get-tuple-element.177, f32[512,512]{0,1:T(8,128)} %get-tuple-element.174, f32[512]{0:T(512)S(1)} %copy-done.128, f32[512]{0:T(512)S(1)} %copy-done.103, f32[512]{0:T(512)S(1)} %copy-done.100, f32[512]{0:T(512)S(1)} %broadcast_multiply_fusion.4, ...), kind=kLoop, calls=%fused_computation.216 | loop fusion | flops 2621440 | bytes 3156480 | tf_op jit(solution)/shard_map/convert_element_type | solution.py:229
  465.5 9.1 %fusion.88 = (bf16[512,784]{0,1:T(8,128)(2,1)}, bf16[512,784]{0,1:T(8,128)(2,1)}) fusion(f32[784,512]{1,0:T(8,128)} %get-tuple-element.170, f32[784,512]{1,0:T(8,128)} %get-tuple-element.172, f32[512,784]{0,1:T(8,128)S(1)} %copy-done.17, f32[512]{0:T(512)S(1)} %copy-done.134, f32[512]{0:T(512)S(1)} %copy-done.111, f32[784]{0:T(1024)S(1)} %copy-done.98, ...), kind=kLoop, calls=%fused_computation.102 | loop fusion | flops 7225344 | bytes 6451968 | tf_op jit(solution)/shard_map/convert_element_type | solution.py:220
  474.6 2.2 copy.173
  476.9 2.2 copy.161
  485.6 2.2 fusion.133
  487.8 2.3 fusion.132
  521.7 3.2 constant_dynamic-update-slice_fusion.16
  537.6 138.9 %reduce-scatter.2.cloned.1.call-done = bf16[1,336,512]{2,1,0:T(8,128)(2,1)} async-done(((bf16[32,336,512]{2,1,0:T(8,128)(2,1)}), bf16[1,336,512]{2,1,0:T(8,128)(2,1)}) %reduce-scatter.2.cloned.1.call-update) | async-done | bytes 344080 | tf_op jit(solution)/shard_map/reduce_scatter | solution.py:500
  (556 shorter events, 136.7 us)
Async XLA Ops:
  7.2 138.7 %copy-start = (bf16[1,784,256]{2,1,0:T(8,128)(2,1)S(1)}, bf16[1,784,256]{2,1,0:T(8,128)(2,1)}, u32[]{:S(2)}) copy-start(bf16[1,784,256]{2,1,0:T(8,128)(2,1)} %param.19) | copy-start | bytes 1204228
  7.2 104.9 %all-gather.3.cloned.1.call-start = ((), (), s32[]{:S(2)}) async-start(), calls=%async_computation.2 | async-start | bytes 11354112 | tf_op jit(solution)/shard_map/all_gather | solution.py:489
  20.3 656.2 %reduce-scatter.2.cloned.1.call-start = ((), (), s32[]{:S(2)}) async-start(), calls=%async_computation.1 | async-start | bytes 11354112 | tf_op jit(solution)/shard_map/reduce_scatter | solution.py:500
  23.1 148.6 %copy-start.158 = (pred[512]{0:T(512)(128)(4,1)}, pred[512]{0:T(512)(128)(4,1)S(1)}, u32[]{:S(2)}) copy-start(pred[512]{0:T(512)(128)(4,1)S(1)} %fusion.193) | copy-start | bytes 1540
  23.1 176.1 %copy-start.108 = (f32[512]{0:T(512)}, f32[512]{0:T(512)S(1)}, u32[]{:S(2)}) copy-start(f32[512]{0:T(512)S(1)} %fusion.199) | copy-start | bytes 6148
  23.8 145.1 %copy-start.42 = (pred[512,512]{0,1:T(8,128)(4,1)}, pred[512,512]{0,1:T(8,128)(4,1)S(1)}, u32[]{:S(2)}) copy-start(pred[512,512]{0,1:T(8,128)(4,1)S(1)} %fusion.154) | copy-start | bytes 786436
  113.3 32.6 %copy-start.22 = (bf16[32,16,512]{2,1,0:T(8,128)(2,1)}, bf16[32,16,512]{2,1,0:T(8,128)(2,1)S(1)}, u32[]{:S(2)}) copy-start(bf16[32,16,512]{2,1,0:T(8,128)(2,1)S(1)} %slice.373) | copy-start | bytes 1572868
  132.6 9.1 %copy-start.32 = (bf16[1,32,16,512]{3,2,0,1:T(8,128)(2,1)}, bf16[1,32,16,512]{3,2,0,1:T(8,128)(2,1)S(1)}, u32[]{:S(2)}) copy-start(bf16[1,32,16,512]{3,2,0,1:T(8,128)(2,1)S(1)} %get-tuple-element.131) | copy-start | bytes 1572868
  145.4 8.4 %copy-start.65 = (bf16[1,32,16,512]{3,2,0,1:T(8,128)(2,1)}, bf16[1,32,16,512]{3,2,0,1:T(8,128)(2,1)S(1)}, u32[]{:S(2)}) copy-start(bf16[1,32,16,512]{3,2,0,1:T(8,128)(2,1)S(1)} %get-tuple-element.133) | copy-start | bytes 1572868
  145.9 7.9 %copy-start.114 = (f32[512]{0:T(512)}, f32[512]{0:T(512)S(1)}, u32[]{:S(2)}) copy-start(f32[512]{0:T(512)S(1)} %get-tuple-element.93) | copy-start | bytes 6148
  155.8 22.0 %copy-start.11 = (bf16[784,512]{0,1:T(8,128)(2,1)}, bf16[784,512]{0,1:T(8,128)(2,1)S(1)}, u32[]{:S(2)}) copy-start(bf16[784,512]{0,1:T(8,128)(2,1)S(1)} %copy.141) | copy-start | bytes 2408452
  161.9 27.1 %copy-start.10 = (bf16[784,512]{0,1:T(8,128)(2,1)}, bf16[784,512]{0,1:T(8,128)(2,1)S(1)}, u32[]{:S(2)}) copy-start(bf16[784,512]{0,1:T(8,128)(2,1)S(1)} %copy.139) | copy-start | bytes 2408452
  177.8 145.9 %copy-start.99 = (f32[512]{0:T(512)}, f32[512]{0:T(512)S(1)}, u32[]{:S(2)}) copy-start(f32[512]{0:T(512)S(1)} %fusion.204) | copy-start | bytes 6148
  189.1 10.1 %copy-start.16 = (f32[512,784]{0,1:T(8,128)S(1)}, f32[512,784]{0,1:T(8,128)}, u32[]{:S(2)}) copy-start(f32[512,784]{0,1:T(8,128)} %get-tuple-element.167) | copy-start | bytes 4816900
  189.1 10.1 %copy-start.90 = (bf16[1,32,16,512]{3,2,0,1:T(8,128)(2,1)S(1)}, bf16[1,32,16,512]{3,2,0,1:T(8,128)(2,1)}, u32[]{:S(2)}) copy-start(bf16[1,32,16,512]{3,2,0,1:T(8,128)(2,1)} %get-tuple-element.132) | copy-start | bytes 1572868
  189.1 10.1 %copy-start.115 = (f32[512]{0:T(512)S(1)}, f32[512]{0:T(512)}, u32[]{:S(2)}) copy-start(f32[512]{0:T(512)} %copy-done.114) | copy-start | bytes 6148
  189.1 10.1 %copy-start.140 = (f32[512]{0:T(512)S(1)}, f32[512]{0:T(512)}, u32[]{:S(2)}) copy-start(f32[512]{0:T(512)} %copy-done.139) | copy-start | bytes 6148
  189.1 10.1 %copy-start.159 = (pred[512]{0:T(512)(128)(4,1)S(1)}, pred[512]{0:T(512)(128)(4,1)}, u32[]{:S(2)}) copy-start(pred[512]{0:T(512)(128)(4,1)} %copy-done.158) | copy-start | bytes 1540
  199.1 8.1 %copy-start.181 = (bf16[8,64,784]{2,1,0:T(8,128)(2,1)}, bf16[8,64,784]{2,1,0:T(8,128)(2,1)S(1)}, u32[]{:S(2)}) copy-start(bf16[8,64,784]{2,1,0:T(8,128)(2,1)S(1)} %fusion.102) | copy-start | bytes 2408452
  199.2 8.4 %copy-start.84 = (bf16[1,32,16,512]{3,2,0,1:T(8,128)(2,1)S(1)}, bf16[1,32,16,512]{3,2,0,1:T(8,128)(2,1)}, u32[]{:S(2)}) copy-start(bf16[1,32,16,512]{3,2,0,1:T(8,128)(2,1)} %get-tuple-element.145) | copy-start | bytes 1572868
  199.2 8.4 %copy-start.86 = (bf16[1,32,16,512]{3,2,0,1:T(8,128)(2,1)S(1)}, bf16[1,32,16,512]{3,2,0,1:T(8,128)(2,1)}, u32[]{:S(2)}) copy-start(bf16[1,32,16,512]{3,2,0,1:T(8,128)(2,1)} %get-tuple-element.146) | copy-start | bytes 1572868
  199.2 8.4 %copy-start.120 = (f32[512]{0:T(512)S(1)}, f32[512]{0:T(512)}, u32[]{:S(2)}) copy-start(f32[512]{0:T(512)} %get-tuple-element.92) | copy-start | bytes 6148
  199.2 8.4 %copy-start.137 = (f32[512]{0:T(512)S(1)}, f32[512]{0:T(512)}, u32[]{:S(2)}) copy-start(f32[512]{0:T(512)} %get-tuple-element.91) | copy-start | bytes 6148
  199.2 8.4 %copy-start.161 = (f32[1024]{0:T(1024)S(1)}, f32[1024]{0:T(1024)}, u32[]{:S(2)}) copy-start(f32[1024]{0:T(1024)} %reshape.736) | copy-start | bytes 12292
  207.2 10.0 %copy-start.14 = (f32[784,512]{1,0:T(8,128)}, f32[784,512]{1,0:T(8,128)S(1)}, u32[]{:S(2)}) copy-start(f32[784,512]{1,0:T(8,128)S(1)} %get-tuple-element.116) | copy-start | bytes 4816900
  207.2 114.0 %copy-start.95 = (f32[784]{0:T(1024)}, f32[784]{0:T(1024)S(1)}, u32[]{:S(2)}) copy-start(f32[784]{0:T(1024)S(1)} %broadcast_multiply_fusion.1) | copy-start | bytes 9412
  207.6 9.6 %copy-start.104 = (f32[784]{0:T(1024)}, f32[784]{0:T(1024)S(1)}, u32[]{:S(2)}) copy-start(f32[784]{0:T(1024)S(1)} %multiply_reduce_fusion.10) | copy-start | bytes 9412
  207.6 113.6 %copy-start.106 = (f32[784]{0:T(1024)}, f32[784]{0:T(1024)S(1)}, u32[]{:S(2)}) copy-start(f32[784]{0:T(1024)S(1)} %fusion.191) | copy-start | bytes 9412
  207.7 9.6 %copy-start.77 = (bf16[32,32,512]{2,1,0:T(8,128)(2,1)S(1)}, bf16[32,32,512]{2,1,0:T(8,128)(2,1)}, u32[]{:S(2)}) copy-start(bf16[32,32,512]{2,1,0:T(8,128)(2,1)} %get-tuple-element.119) | copy-start | bytes 3145732
  207.7 9.6 %copy-start.135 = (f32[512]{0:T(512)S(1)}, f32[512]{0:T(512)}, u32[]{:S(2)}) copy-start(f32[512]{0:T(512)} %get-tuple-element.90) | copy-start | bytes 6148
  220.1 89.8 %copy-start.97 = (f32[784]{0:T(1024)}, f32[784]{0:T(1024)S(1)}, u32[]{:S(2)}) copy-start(f32[784]{0:T(1024)S(1)} %fusion.192) | copy-start | bytes 9412
  231.7 31.3 %copy-start.2 = (f32[8,512,784]{1,2,0:T(8,128)}, f32[8,512,784]{1,2,0:T(8,128)S(1)}, u32[]{:S(2)}) copy-start(f32[8,512,784]{1,2,0:T(8,128)S(1)} %get-tuple-element.179) | copy-start | bytes 38535172
  256.0 67.7 %copy-start.112 = (f32[512]{0:T(512)}, f32[512]{0:T(512)S(1)}, u32[]{:S(2)}) copy-start(f32[512]{0:T(512)S(1)} %negate_multiply_fusion.5) | copy-start | bytes 6148
  265.5 42.6 %copy-start.39 = (bf16[8,64,784]{2,1,0:T(8,128)(2,1)}, bf16[8,64,784]{2,1,0:T(8,128)(2,1)S(1)}, u32[]{:S(2)}) copy-start(bf16[8,64,784]{2,1,0:T(8,128)(2,1)S(1)} %fusion.106) | copy-start | bytes 2408452
  321.2 10.2 %slice-start = ((s8[8388608]{0:T(1024)(128)(4,1)}), s8[4194304]{0:T(1024)(128)(4,1)S(1)}, s32[]{:S(2)}) async-start(s8[8388608]{0:T(1024)(128)(4,1)} %bitcast.393), calls=%async_computation.3 | async-start | bytes 8388608
  334.5 14.4 %copy-start.48 = (bf16[512,512]{0,1:T(8,128)(2,1)S(1)}, bf16[512,512]{0,1:T(8,128)(2,1)}, u32[]{:S(2)}) copy-start(bf16[512,512]{0,1:T(8,128)(2,1)} %convolution_convert_fusion.20) | copy-start | bytes 1572868
  348.9 14.4 %copy-start.105 = (f32[784]{0:T(1024)S(1)}, f32[784]{0:T(1024)}, u32[]{:S(2)}) copy-start(f32[784]{0:T(1024)} %copy-done.104) | copy-start | bytes 9412
  348.9 14.4 %copy-start.170 = (f32[784]{0:T(1024)S(1)}, f32[784]{0:T(1024)}, u32[]{:S(2)}) copy-start(f32[784]{0:T(1024)} %get-tuple-element.67) | copy-start | bytes 9412
  348.9 14.4 %copy-start.96 = (f32[784]{0:T(1024)S(1)}, f32[784]{0:T(1024)}, u32[]{:S(2)}) copy-start(f32[784]{0:T(1024)} %copy-done.95) | copy-start | bytes 9412
  348.9 14.4 %copy-start.107 = (f32[784]{0:T(1024)S(1)}, f32[784]{0:T(1024)}, u32[]{:S(2)}) copy-start(f32[784]{0:T(1024)} %copy-done.106) | copy-start | bytes 9412
  349.0 14.4 %copy-start.121 = (f32[512]{0:T(512)S(1)}, f32[512]{0:T(512)}, u32[]{:S(2)}) copy-start(f32[512]{0:T(512)} %get-tuple-element.92) | copy-start | bytes 6148
  370.7 11.8 %copy-start.94 = (f32[8,784]{1,0:T(8,128)S(1)}, f32[8,784]{1,0:T(8,128)}, u32[]{:S(2)}) copy-start(f32[8,784]{1,0:T(8,128)} %log_add_fusion) | copy-start | bytes 75268
  394.6 31.3 %copy-start.13 = (bf16[784,512]{0,1:T(8,128)(2,1)S(1)}, bf16[784,512]{0,1:T(8,128)(2,1)}, u32[]{:S(2)}) copy-start(bf16[784,512]{0,1:T(8,128)(2,1)} %copy.140) | copy-start | bytes 2408452
  426.0 31.7 %copy-start.100 = (f32[512]{0:T(512)S(1)}, f32[512]{0:T(512)}, u32[]{:S(2)}) copy-start(f32[512]{0:T(512)} %copy-done.99) | copy-start | bytes 6148
  426.0 31.7 %copy-start.103 = (f32[512]{0:T(512)S(1)}, f32[512]{0:T(512)}, u32[]{:S(2)}) copy-start(f32[512]{0:T(512)} %get-tuple-element.87) | copy-start | bytes 6148
  426.0 31.7 %copy-start.109 = (f32[512]{0:T(512)S(1)}, f32[512]{0:T(512)}, u32[]{:S(2)}) copy-start(f32[512]{0:T(512)} %copy-done.108) | copy-start | bytes 6148
  426.0 31.7 %copy-start.128 = (f32[512]{0:T(512)S(1)}, f32[512]{0:T(512)}, u32[]{:S(2)}) copy-start(f32[512]{0:T(512)} %get-tuple-element.86) | copy-start | bytes 6148
  426.0 31.7 %copy-start.160 = (pred[512]{0:T(512)(128)(4,1)S(1)}, pred[512]{0:T(512)(128)(4,1)}, u32[]{:S(2)}) copy-start(pred[512]{0:T(512)(128)(4,1)} %copy-done.158) | copy-start | bytes 1540
  (145 other events, 422.0 us)
Sparse Core Ops, SparseCore 0:
  20.4 91.5 all-gather.2
  534.4 142.0 reduce-scatter.1

commit v2 on v1

v2 whole, which is shorter than its diff:
```python
from functools import partial
import math

import jax
import jax.numpy as jnp
import numpy as np
from jax import lax
from jax.experimental import pallas as pl
from jax.experimental.pallas import tpu as pltpu
from jax.sharding import PartitionSpec as P

HEADS = 8
VOCAB = 32
AXES = ("wide", "narrow")
LOW = jnp.bfloat16
WIDE = jnp.float32

MISC, ENC, ENC_IN, ENC_OUT, SELF, CROSS, DEC_IN, DEC_OUT, PIECES = 0, 1, 5, 7, 9, 13, 17, 19, 21
BN, AFFINE, ENC_VEC, DEC_VEC, TABLE, VECTOR_ROWS = 0, 2, 4, 9, 16, 128


def dot_nn(left, right):
    return lax.dot_general(left, right, (((1,), (0,)), ((), ())), preferred_element_type=WIDE)


def dot_nt(left, right):
    return lax.dot_general(left, right, (((1,), (1,)), ((), ())), preferred_element_type=WIDE)


def dot_tn(left, right):
    return lax.dot_general(left, right, (((0,), (0,)), ((), ())), preferred_element_type=WIDE)


def position_table(rows, width):
    place = np.arange(rows, dtype=np.float64)[:, None]
    column = np.arange(width)
    inverse = np.exp(-(2 * (column // 2)) / width * math.log(10000.0))
    angle = place * inverse[None, :]
    return np.where((column % 2 == 0)[None, :], np.sin(angle), np.cos(angle)).astype(np.float32)


def norm_stats(value):
    centred = value - jnp.mean(value, axis=1, keepdims=True)
    scale = lax.rsqrt(jnp.mean(centred * centred, axis=1, keepdims=True) + 1e-05)
    return centred * scale, scale


def norm_back(grad, normal, scale, gain):
    inner = grad * gain
    return scale * (
        inner
        - jnp.mean(inner, axis=1, keepdims=True)
        - normal * jnp.mean(inner * normal, axis=1, keepdims=True)
    )


def col_sum(value):
    return jnp.sum(value, axis=0, keepdims=True)


def gauss_share(value):
    return 0.5 + 0.5 * lax.erf(value * math.sqrt(0.5))


def gauss_slope(value):
    return jnp.exp(value * value * -0.5) * (1.0 / math.sqrt(2.0 * math.pi))


def two_tiles(count):
    top = (count // 2 + 15) // 16 * 16
    return [(0, top), (top, count - top)]


def pick(mask, half, value):
    zero = jnp.zeros((), value.dtype)
    return jnp.where(mask, value, zero) if half == 0 else jnp.where(mask, zero, value)


def first_half(shape):
    return lax.broadcasted_iota(jnp.int32, shape, 1) < shape[1] // 2


def attend(q_ref, k_ref, v_ref, o_ref, lse_ref, tiles, length):
    slab = 128
    half_scale = LOW(0.125)

    def pair(index, _):
        cols = pl.ds(pl.multiple_of(index * slab, slab), slab)
        for start, size, keys in tiles:
            rows = pl.ds(start, size)
            k = k_ref[0:keys, cols]
            v = v_ref[0:keys, cols]
            left_k = first_half(v.shape)
            q = q_ref[rows, cols] * half_scale
            left = first_half(q.shape)
            outs, tops, sums = [], [], []
            for half in range(2):
                s = dot_nt(pick(left, half, q), k)
                if length is not None:
                    s = mask_scores(s, start, length)
                top = jnp.max(s, axis=1, keepdims=True)
                p = jnp.exp(s - top).astype(LOW)
                ones = jnp.ones((), LOW)
                full = jnp.where(left_k, v, ones) if half == 0 else jnp.where(left_k, ones, v)
                out = dot_nn(p, full)
                outs.append(out)
                tops.append(top)
                sums.append(out[:, 64:65] if half == 0 else out[:, 0:1])
            o_ref[rows, cols] = jnp.where(left, outs[0] / sums[0], outs[1] / sums[1]).astype(LOW)
            lane = lax.broadcasted_iota(jnp.int32, (size, slab), 1) - 2 * index
            kept = jnp.where(lane == 0, tops[0] + jnp.log(sums[0]), lse_ref[rows, :])
            lse_ref[rows, :] = jnp.where(lane == 1, tops[1] + jnp.log(sums[1]), kept)
        return 0

    lax.fori_loop(0, HEADS // 2, pair, 0)


def mask_scores(s, start, length):
    query = lax.broadcasted_iota(jnp.int32, s.shape, 0) + start
    key = lax.broadcasted_iota(jnp.int32, s.shape, 1)
    return jnp.where((key <= query) & (key < length), s, -1e30)


def attend_back(
    q_ref, k_ref, v_ref, lse_ref, do_ref, dq_ref, dk_ref, dv_ref, dk_acc, dv_acc, tiles, length
):
    slab = 128
    half_scale = LOW(0.125)
    total = k_ref.shape[0]

    def pair(index, _):
        cols = pl.ds(pl.multiple_of(index * slab, slab), slab)
        first = True
        for start, size, keys in sorted(tiles, key=lambda t: -t[2]):
            rows = pl.ds(start, size)
            k = k_ref[0:keys, cols]
            v = v_ref[0:keys, cols]
            q = q_ref[rows, cols] * half_scale
            do = do_ref[rows, cols]
            lane = lax.broadcasted_iota(jnp.int32, (size, slab), 1) - 2 * index
            left = first_half(q.shape)
            grads, dks, dvs = [], [], []
            for half in range(2):
                qh, doh = pick(left, half, q), pick(left, half, do)
                s = dot_nt(qh, k)
                if length is not None:
                    s = mask_scores(s, start, length)
                lse = jnp.sum(jnp.where(lane == half, lse_ref[rows, :], 0.0), axis=1, keepdims=True)
                p = jnp.exp(s - lse)
                mixed = p * dot_nt(doh, v)
                ds = (mixed - p * jnp.sum(mixed, axis=1, keepdims=True)).astype(LOW)
                p = p.astype(LOW)
                grads.append(dot_nn(ds, k))
                dks.append(dot_tn(qh, ds))
                dvs.append(dot_tn(doh, p))
            dq_ref[rows, cols] = (jnp.where(left, grads[0], grads[1]) * 0.125).astype(LOW)
            if first:
                dk_acc[:, 0:keys] = dks[0] + dks[1]
                dv_acc[:, 0:keys] = dvs[0] + dvs[1]
            else:
                dk_acc[:, 0:keys] += dks[0] + dks[1]
                dv_acc[:, 0:keys] += dvs[0] + dvs[1]
            first = False
        dk_ref[0:total, cols] = dk_acc[:, 0:total].T.astype(LOW)
        dv_ref[0:total, cols] = dv_acc[:, 0:total].T.astype(LOW)
        return 0

    lax.fori_loop(0, HEADS // 2, pair, 0)


def layer_kernel(
    feat,
    ids,
    lens,
    cot,
    pos,
    w,
    decoded,
    gfeat,
    g,
    x,
    xl,
    q,
    k,
    v,
    o,
    lse,
    r2,
    ml,
    e,
    el,
    qs,
    ks,
    vs,
    os,
    lses,
    s2,
    sl,
    qc,
    kc,
    vc,
    oc,
    lsec,
    fl,
    hid,
    dpre,
    gl,
    do,
    dq,
    dk,
    dv,
    dm,
    dk_acc,
    dv_acc,
    vec,
    gvec,
):
    patches, width = x.shape
    tags = e.shape[0]
    channels = feat.shape[1]
    hidden = hid.shape[1]
    wide_tiles = two_tiles(patches)
    tag_tiles = two_tiles(tags)
    pltpu.sync_copy(pos, dm)
    vec[...] = w[MISC, :, channels : channels + VECTOR_ROWS].astype(WIDE).T
    gvec[...] = jnp.zeros_like(gvec)
    length = lens[0:1, 0:1]

    def row(index):
        return vec[index : index + 1, :]

    def hidden_bias(index):
        return jnp.concatenate([row(index), row(index + 1)], axis=1)

    vocab = VOCAB
    enc_hidden, dec_hidden = TABLE + vocab, TABLE + vocab + 2
    bn_scale = lax.rsqrt(row(BN + 1) + 1e-05)

    def encode_rows(start, size):
        rows = pl.ds(start, size)
        projected = dot_nt(feat[rows, :], w[MISC, :, 0:channels])
        begin = (projected - row(BN)) * bn_scale * row(AFFINE) + row(AFFINE + 1) + dm[rows, :]
        x[rows, :] = begin
        low = begin.astype(LOW)
        xl[rows, :] = low
        q[rows, :] = dot_nn(low, w[ENC]).astype(LOW)
        k[rows, :] = dot_nn(low, w[ENC + 1]).astype(LOW)
        v[rows, :] = dot_nn(low, w[ENC + 2]).astype(LOW)

    for tile in wide_tiles:
        encode_rows(*tile)
    attend(q, k, v, o, lse, [(0, patches, patches)], None)

    def encode_feed(start, size):
        rows = pl.ds(start, size)
        resid = x[rows, :] + dot_nn(o[rows, :], w[ENC + 3])
        x[rows, :] = resid
        normal, _scale = norm_stats(resid)
        first = normal * row(ENC_VEC) + row(ENC_VEC + 1)
        low = first.astype(LOW)
        total = first + row(ENC_VEC + 2)
        for half in range(2):
            pre = dot_nn(low, w[ENC_IN + half]) + row(enc_hidden + half)
            act = (pre * gauss_share(pre)).astype(LOW)
            total = total + dot_nn(act, w[ENC_OUT + half])
        r2[rows, :] = total
        normal, _scale = norm_stats(total)
        memory = normal * row(ENC_VEC + 3) + row(ENC_VEC + 4)
        ml[rows, :] = memory.astype(LOW)
        kc[rows, :] = dot_nn(ml[rows, :], w[CROSS + 1]).astype(LOW)
        vc[rows, :] = dot_nn(ml[rows, :], w[CROSS + 2]).astype(LOW)

    for tile in wide_tiles:
        encode_feed(*tile)

    onehot = (
        lax.broadcasted_iota(jnp.int32, (vocab, tags), 0) == ids[0:1, :]
    ).astype(WIDE).astype(LOW)
    table = vec[TABLE : TABLE + vocab, :].astype(LOW)
    e[...] = dot_tn(onehot, table) + dm[0:tags, :]
    el[...] = e[...].astype(LOW)
    qs[...] = dot_nn(el[...], w[SELF]).astype(LOW)
    ks[...] = dot_nn(el[...], w[SELF + 1]).astype(LOW)
    vs[...] = dot_nn(el[...], w[SELF + 2]).astype(LOW)
    causal_tiles = [(start, size, start + size) for start, size in tag_tiles]
    attend(qs, ks, vs, os, lses, causal_tiles, length)

    def decode_rows(start, size):
        rows = pl.ds(start, size)
        resid = e[rows, :] + dot_nn(os[rows, :], w[SELF + 3])
        e[rows, :] = resid
        normal, _scale = norm_stats(resid)
        second = normal * row(DEC_VEC) + row(DEC_VEC + 1)
        s2[rows, :] = second
        sl[rows, :] = second.astype(LOW)
        qc[rows, :] = dot_nn(sl[rows, :], w[CROSS]).astype(LOW)

    for tile in tag_tiles:
        decode_rows(*tile)
    attend(qc, kc, vc, oc, lsec, [(0, tags, patches)], None)

    def decode_feed(start, size):
        rows = pl.ds(start, size)
        resid = s2[rows, :] + dot_nn(oc[rows, :], w[CROSS + 3])
        normal_two, scale_two = norm_stats(resid)
        third = normal_two * row(DEC_VEC + 2) + row(DEC_VEC + 3)
        low = third.astype(LOW)
        fl[rows, :] = low
        total = third + row(DEC_VEC + 4)
        kept = []
        for half in range(2):
            pre = dot_nn(low, w[DEC_IN + half]) + row(dec_hidden + half)
            share = gauss_share(pre)
            act = (pre * share).astype(LOW)
            hid[rows, half * width : (half + 1) * width] = act
            total = total + dot_nn(act, w[DEC_OUT + half])
            kept.append(share + pre * gauss_slope(pre))
        normal, scale = norm_stats(total)
        place = lax.broadcasted_iota(jnp.int32, (size, 1), 0) + start
        live = jnp.where(place < length, 1.0, 0.0)
        decoded[rows, :] = ((normal * row(DEC_VEC + 5) + row(DEC_VEC + 6)) * live).astype(LOW)
        grad = cot[rows, :].astype(WIDE) * live
        gvec[DEC_VEC + 5 : DEC_VEC + 6, :] += col_sum(grad * normal)
        gvec[DEC_VEC + 6 : DEC_VEC + 7, :] += col_sum(grad)
        grad = norm_back(grad, normal, scale, row(DEC_VEC + 5))
        gvec[DEC_VEC + 4 : DEC_VEC + 5, :] += col_sum(grad)
        grad_low = grad.astype(LOW)
        gl[rows, :] = grad_low
        for half in range(2):
            back = dot_nt(grad_low, w[DEC_OUT + half]) * kept[half]
            gvec[dec_hidden + half : dec_hidden + half + 1, :] += col_sum(back)
            back = back.astype(LOW)
            dpre[rows, half * width : (half + 1) * width] = back
            grad = grad + dot_nt(back, w[DEC_IN + half])
        gvec[DEC_VEC + 2 : DEC_VEC + 3, :] += col_sum(grad * normal_two)
        gvec[DEC_VEC + 3 : DEC_VEC + 4, :] += col_sum(grad)
        grad = norm_back(grad, normal_two, scale_two, row(DEC_VEC + 2))
        s2[rows, :] = grad
        dq[rows, :] = grad.astype(LOW)
        do[rows, :] = dot_nt(dq[rows, :], w[CROSS + 3]).astype(LOW)

    for tile in tag_tiles:
        decode_feed(*tile)
    tag_rows = slice(0, tags)

    def weight_grad(piece, left, right):
        g[piece] = dot_tn(left, right).astype(LOW)

    for half in range(2):
        cols = slice(half * width, (half + 1) * width)
        weight_grad(DEC_IN + half, fl[tag_rows, :], dpre[tag_rows, cols])
        weight_grad(DEC_OUT + half, hid[tag_rows, cols], gl[tag_rows, :])
    weight_grad(CROSS + 3, oc[...], dq[tag_rows, :])
    attend_back(
        qc, kc, vc, lsec, do, dq, dk, dv, dk_acc, dv_acc, [(0, tags, patches)], None
    )
    weight_grad(CROSS, sl[...], dq[tag_rows, :])
    weight_grad(CROSS + 1, ml[...], dk[...])
    weight_grad(CROSS + 2, ml[...], dv[...])

    def cross_memory(start, size):
        rows = pl.ds(start, size)
        dm[rows, :] = dot_nt(dk[rows, :], w[CROSS + 1]) + dot_nt(dv[rows, :], w[CROSS + 2])

    for tile in wide_tiles:
        cross_memory(*tile)

    def self_rows(start, size):
        rows = pl.ds(start, size)
        grad = s2[rows, :] + dot_nt(dq[rows, :], w[CROSS])
        normal, scale = norm_stats(e[rows, :])
        gvec[DEC_VEC : DEC_VEC + 1, :] += col_sum(grad * normal)
        gvec[DEC_VEC + 1 : DEC_VEC + 2, :] += col_sum(grad)
        grad = norm_back(grad, normal, scale, row(DEC_VEC))
        s2[rows, :] = grad
        gl[rows, :] = grad.astype(LOW)
        do[rows, :] = dot_nt(gl[rows, :], w[SELF + 3]).astype(LOW)

    for tile in tag_tiles:
        self_rows(*tile)
    weight_grad(SELF + 3, os[...], gl[tag_rows, :])
    attend_back(qs, ks, vs, lses, do, dq, dk, dv, dk_acc, dv_acc, causal_tiles, length)
    weight_grad(SELF, el[...], dq[tag_rows, :])
    weight_grad(SELF + 1, el[...], dk[tag_rows, :])
    weight_grad(SELF + 2, el[...], dv[tag_rows, :])
    grad = (
        s2[...]
        + dot_nt(dq[tag_rows, :], w[SELF])
        + dot_nt(dk[tag_rows, :], w[SELF + 1])
        + dot_nt(dv[tag_rows, :], w[SELF + 2])
    )
    high = grad.astype(LOW)
    rest = (grad - high.astype(WIDE)).astype(LOW)
    gvec[TABLE : TABLE + vocab, :] = dot_nn(onehot, high) + dot_nn(onehot, rest)

    def encode_back(start, size):
        rows = pl.ds(start, size)
        normal, scale = norm_stats(r2[rows, :])
        grad = dm[rows, :]
        gvec[ENC_VEC + 3 : ENC_VEC + 4, :] += col_sum(grad * normal)
        gvec[ENC_VEC + 4 : ENC_VEC + 5, :] += col_sum(grad)
        grad = norm_back(grad, normal, scale, row(ENC_VEC + 3))
        gvec[ENC_VEC + 2 : ENC_VEC + 3, :] += col_sum(grad)
        grad_low = grad.astype(LOW)
        gl[rows, :] = grad_low
        normal, scale = norm_stats(x[rows, :])
        low = (normal * row(ENC_VEC) + row(ENC_VEC + 1)).astype(LOW)
        fl[rows, :] = low
        for half in range(2):
            cols = slice(half * width, (half + 1) * width)
            pre = dot_nn(low, w[ENC_IN + half]) + row(enc_hidden + half)
            share = gauss_share(pre)
            hid[rows, cols] = (pre * share).astype(LOW)
            back = dot_nt(grad_low, w[ENC_OUT + half]) * (share + pre * gauss_slope(pre))
            gvec[enc_hidden + half : enc_hidden + half + 1, :] += col_sum(back)
            back = back.astype(LOW)
            dpre[rows, cols] = back
            grad = grad + dot_nt(back, w[ENC_IN + half])
        gvec[ENC_VEC : ENC_VEC + 1, :] += col_sum(grad * normal)
        gvec[ENC_VEC + 1 : ENC_VEC + 2, :] += col_sum(grad)
        grad = norm_back(grad, normal, scale, row(ENC_VEC))
        dm[rows, :] = grad
        dq[rows, :] = grad.astype(LOW)
        do[rows, :] = dot_nt(dq[rows, :], w[ENC + 3]).astype(LOW)

    for tile in wide_tiles:
        encode_back(*tile)
    for half in range(2):
        cols = slice(half * width, (half + 1) * width)
        weight_grad(ENC_IN + half, fl[...], dpre[:, cols])
        weight_grad(ENC_OUT + half, hid[:, cols], gl[...])
    weight_grad(ENC + 3, o[...], dq[...])
    halves = [(start, size, patches) for start, size in wide_tiles]
    attend_back(q, k, v, lse, do, dq, dk, dv, dk_acc, dv_acc, halves, None)
    weight_grad(ENC, xl[...], dq[...])
    weight_grad(ENC + 1, xl[...], dk[...])
    weight_grad(ENC + 2, xl[...], dv[...])

    def project_back(start, size):
        rows = pl.ds(start, size)
        grad = (
            dm[rows, :]
            + dot_nt(dq[rows, :], w[ENC])
            + dot_nt(dk[rows, :], w[ENC + 1])
            + dot_nt(dv[rows, :], w[ENC + 2])
        )
        projected = dot_nt(feat[rows, :], w[MISC, :, 0:channels])
        gvec[AFFINE : AFFINE + 1, :] += col_sum(grad * (projected - row(BN)) * bn_scale)
        gvec[AFFINE + 1 : AFFINE + 2, :] += col_sum(grad)
        low = (grad * (bn_scale * row(AFFINE))).astype(LOW)
        gl[rows, :] = low
        gfeat[rows, :] = dot_nn(low, w[MISC, :, 0:channels])

    for tile in wide_tiles:
        project_back(*tile)
    g[MISC, :, 0:channels] = dot_tn(gl[...], feat[...]).astype(LOW)
    g[MISC, :, channels : channels + VECTOR_ROWS] = gvec[...].T.astype(LOW)
    g[MISC, :, channels + VECTOR_ROWS :] = jnp.zeros(
        (width, width - channels - VECTOR_ROWS), LOW
    )


def layer_call(features, ids, length, cot, stack, hidden):
    patches, channels = features.shape
    tags, width = cot.shape
    lens = jnp.broadcast_to(length.reshape(1, 1), (8, 128))
    pos = jnp.asarray(position_table(max(patches, tags), width))
    wide = lambda *shape: pltpu.VMEM(shape, WIDE)
    low = lambda *shape: pltpu.VMEM(shape, LOW)
    vmem = pl.BlockSpec(memory_space=pltpu.VMEM)
    return pl.pallas_call(
        layer_kernel,
        in_specs=[vmem, vmem, vmem, vmem, pl.BlockSpec(memory_space=pl.ANY), vmem],
        out_shape=(
            jax.ShapeDtypeStruct((tags, width), LOW),
            jax.ShapeDtypeStruct((patches, channels), WIDE),
            jax.ShapeDtypeStruct(stack.shape, LOW),
        ),
        scratch_shapes=[
            wide(patches, width),
            low(patches, width),
            low(patches, width),
            low(patches, width),
            low(patches, width),
            low(patches, width),
            wide(patches, 128),
            wide(patches, width),
            low(patches, width),
            wide(tags, width),
            low(tags, width),
            low(tags, width),
            low(tags, width),
            low(tags, width),
            low(tags, width),
            wide(tags, 128),
            wide(tags, width),
            low(tags, width),
            low(tags, width),
            low(patches, width),
            low(patches, width),
            low(tags, width),
            wide(tags, 128),
            low(patches, width),
            low(patches, hidden),
            low(patches, hidden),
            low(patches, width),
            low(patches, width),
            low(patches, width),
            low(patches, width),
            low(patches, width),
            wide(patches, width),
            wide(128, patches),
            wide(128, patches),
            wide(VECTOR_ROWS, width),
            wide(VECTOR_ROWS, width),
        ],
        compiler_params=pltpu.CompilerParams(vmem_limit_bytes=63 << 20),
        name="layers",
    )(features, ids, lens, cot, pos, stack)


def pack_parameters(
    proj_weight,
    bn_given,
    bn_affine,
    enc_attn,
    enc_vec,
    enc_ffn_in,
    enc_hidden_bias,
    enc_ffn_out,
    tag_table,
    dec_self,
    dec_cross,
    dec_vec,
    dec_ffn_in,
    dec_hidden_bias,
    dec_ffn_out,
):
    rows = proj_weight.shape[1]
    width = enc_attn.shape[2]
    columns = jnp.concatenate(
        [
            proj_weight,
            bn_given,
            bn_affine,
            enc_vec,
            dec_vec,
            tag_table,
            enc_hidden_bias.reshape(-1, rows),
            dec_hidden_bias.reshape(-1, rows),
        ],
        axis=0,
    )
    columns = jnp.pad(columns, ((0, width - columns.shape[0]), (0, 0))).T

    def halves(matrix):
        split = matrix.reshape(rows, -1, 2, rows)
        return split.transpose(2, 0, 1, 3).reshape(2, rows, width)

    return jnp.concatenate(
        [
            columns[None],
            enc_attn,
            halves(enc_ffn_in),
            enc_ffn_out.reshape(2, rows, width),
            dec_self,
            dec_cross,
            halves(dec_ffn_in),
            dec_ffn_out.reshape(2, rows, width),
        ],
        axis=0,
    )


def unpack_gradients(share, channels, vocab):
    share = share.astype(WIDE)
    rows, width = share.shape[1:]
    columns = share[MISC, :, 0 : channels + VECTOR_ROWS].T
    vectors = columns[channels:]

    def whole(pair):
        split = pair.reshape(2, rows, -1, rows)
        return split.transpose(1, 2, 0, 3).reshape(rows, 2 * width)

    at = TABLE + vocab
    return (
        columns[:channels],
        vectors[AFFINE : AFFINE + 2],
        share[ENC:ENC_IN],
        vectors[ENC_VEC:DEC_VEC],
        whole(share[ENC_IN:ENC_OUT]),
        vectors[at : at + 2].reshape(-1),
        share[ENC_OUT:SELF].reshape(2 * rows, width),
        vectors[TABLE:at],
        share[SELF:CROSS],
        share[CROSS:DEC_IN],
        vectors[DEC_VEC:TABLE],
        whole(share[DEC_IN:DEC_OUT]),
        vectors[at + 2 : at + 4].reshape(-1),
        share[DEC_OUT:PIECES].reshape(2 * rows, width),
    )


def body(features, tag_ids, tag_lengths, out_cot, *parameters):
    channels, vocab = parameters[0].shape[0], parameters[8].shape[0]
    hidden = parameters[5].shape[1]
    packed = pack_parameters(*parameters)
    stack = lax.all_gather(packed, AXES, axis=1, tiled=True)
    decoded, grad_features, grads = layer_call(
        features[0], tag_ids, tag_lengths, out_cot[0], stack, hidden
    )
    share = lax.psum_scatter(grads, AXES, scatter_dimension=1, tiled=True)
    return (decoded[None], grad_features[None], *unpack_gradients(share, channels, vocab))


def solution(mesh):
    placed = (
        P(("wide", "narrow"), None, None),
        P(("wide", "narrow"), None),
        P(("wide", "narrow")),
        P(("wide", "narrow"), None, None),
        P(None, ("wide", "narrow")),
        P(None, ("wide", "narrow")),
        P(None, ("wide", "narrow")),
        P(None, ("wide", "narrow"), None),
        P(None, ("wide", "narrow")),
        P(("wide", "narrow"), None),
        P(("wide", "narrow")),
        P(("wide", "narrow"), None),
        P(None, ("wide", "narrow")),
        P(None, ("wide", "narrow"), None),
        P(None, ("wide", "narrow"), None),
        P(None, ("wide", "narrow")),
        P(("wide", "narrow"), None),
        P(("wide", "narrow")),
        P(("wide", "narrow"), None),
    )
    return jax.shard_map(
        body,
        mesh=mesh,
        in_specs=placed,
        out_specs=(
            P(("wide", "narrow"), None, None),
            P(("wide", "narrow"), None, None),
            P(None, ("wide", "narrow")),
            P(None, ("wide", "narrow")),
            P(None, ("wide", "narrow"), None),
            P(None, ("wide", "narrow")),
            P(("wide", "narrow"), None),
            P(("wide", "narrow")),
            P(("wide", "narrow"), None),
            P(None, ("wide", "narrow")),
            P(None, ("wide", "narrow"), None),
            P(None, ("wide", "narrow"), None),
            P(None, ("wide", "narrow")),
            P(("wide", "narrow"), None),
            P(("wide", "narrow")),
            P(("wide", "narrow"), None),
        ),
        check_vma=False,
    )
```

time: 701 us -> 484 us (0.69)
  matrix products: 302 us -> 0 us
  Pallas kernels: 0 us -> 110 us
  waiting for transfers between devices: 227 us -> 328 us
  local copies, waits for them, and re-layouts: 102 us -> 25.6 us
  other arithmetic: 42.9 us -> 1.04 us
    dot_general x71 -> x0, matrix products: 302 us -> none  [the longest x3 66.3 us: attend_backward(): jnp.einsum('hqk,qhd->khd', grad_raw, split_heads(query_rows), preferred_e...]
    pallas_call x0 -> x1, Pallas kernels: none -> 110 us  [layer_call(): pl.pallas_call(layer_kernel, in_specs=[vmem, vmem, vmem, vmem, pl.BlockSp...]
    reduce_scatter x1, waiting for transfers between devices: 139 us -> 237 us  [body(): share = lax.psum_scatter(grads, AXES, scatter_dimension=1, tiled=True)]
    unnamed x407 -> x16, local copies, waits for them, and re-layouts: 39.5 us -> 9.04 us
    convert_element_type x10 -> x0, local copies, waits for them, and re-layouts: 18.3 us -> none  [the longest x2 3.41 us: ffn_forward(): pre_act = product(inputs_low, weight_in) + hidden_bias.astype(jnp.float32)]
    reduce_sum x16 -> x0, other arithmetic: 18.3 us -> none  [the longest x3 7.96 us: attend_forward(): row_total = jnp.sum(raised, axis=-1, keepdims=True)]
    convert_element_type x6 -> x1, other arithmetic: 19.2 us -> 1.04 us  [unpack_gradients(): share = share.astype(WIDE)]
    slice x19 -> x9, local copies, waits for them, and re-layouts: 22.3 us -> 4.79 us  [the longest x1 1.65 us: unpack_gradients(): share[CROSS:DEC_IN]]
  transfers between devices with their start and end apart: 2 -> 2, of which waited for: 2 -> 2; matrix products, arithmetic and copies ran while one was open for 1% -> 0% of each run, Pallas kernels for 0% -> 0%
where the time goes in v2:
time: 484 us; the launch traced here: 480 us
  waiting for transfers between devices  328 us (68%)
  Pallas kernels  110 us (23%)
  local copies, waits for them, and re-layouts  25.6 us (5%)
  between operations  15.1 us (3%)
    reduce_scatter x1, waiting for transfers between devices, body(): share = lax.psum_scatter(grads, AXES, scatter_dimension=1, tiled=True)  237 us
    pallas_call x1, Pallas kernels, layer_call(): pl.pallas_call(layer_kernel, in_specs=[vmem, vmem, vmem, vmem, pl.BlockSp...  110 us
    all_gather x1, waiting for transfers between devices, body(): stack = lax.all_gather(packed, AXES, axis=1, tiled=True)  90.9 us
  transfers between devices with their start and end apart: 2, of which 2 were waited for; matrix products, arithmetic and copies ran while one was open for 0% of the time, Pallas kernels for 0%

profile of v2, /device:TPU:0, one launch (start us, length us, event | category | flops | bytes accessed | tf_op | source)
XLA Modules:
  0.0 480.3 jit_solution(2007796652956859809)
XLA Ops:
  7.2 0.0 all-gather.2.cloned.1.call-start
  7.2 0.7 reshape.82
  8.0 0.7 reshape.83
  8.7 0.1 copy.56
  8.8 0.1 copy.55
  8.9 0.7 copy.51
  9.6 0.7 copy.52
  10.4 0.8 copy.53
  11.2 0.8 copy.54
  11.9 1.0 reshape.84
  13.0 0.3 reshape.85
  13.3 1.0 reshape.87
  14.3 0.3 reshape.88
  14.6 0.8 concatenate.6
  15.5 0.8 constant_dynamic-update-slice_fusion.6
  16.3 0.8 constant_dynamic-update-slice_fusion.4
  17.1 0.8 constant_dynamic-update-slice_fusion.3
  17.9 0.8 constant_dynamic-update-slice_fusion.2
  18.8 0.8 constant_dynamic-update-slice_fusion
  19.5 0.7 copy-done
  20.2 0.0 all-gather.2.cloned.1.call-update
  20.3 0.0 reduce-scatter.2.cloned.1.call-start
  21.0 90.9 %all-gather.2.cloned.1.call-done.w = bf16[21,512,512]{2,1,0:T(8,128)(2,1)} async-done(((bf16[21,16,512]{2,1,0:T(8,128)(2,1)}), bf16[21,512,512]{2,1,0:T(8,128)(2,1)}) %all-gather.2.cloned.1.call-update) | async-done | bytes 11010064 | tf_op jit(solution)/shard_map/all_gather | solution.py:608
  111.9 0.6 broadcast_in_dim.17.lens
  112.5 110.2 %layers.1 = (bf16[512,512]{1,0:T(8,128)(2,1)}, f32[784,256]{1,0:T(8,128)}, bf16[21,512,512]{2,1,0:T(8,128)(2,1)}) custom-call(bf16[784,256]{1,0:T(8,128)(2,1)} %bitcast.31, s32[1,512]{1,0:T(1,128)} %ids.1, s32[8,128]{1,0:T(8,128)} %broadcast_in_dim.17.lens, bf16[512,512]{1,0:T(8,128)(2,1)} %bitcast.30, f32[784,512]{1,0:T(8,128)} %constant.5.clone.pos, ...), custom_call_target="tpu_custom_call" | custom-call | tf_op jit(solution)/shard_map/layers/pallas_call | solution.py:471
  222.7 0.0 reduce-scatter.2.cloned.1.call-update
  222.7 237.4 %reduce-scatter.2.cloned.1.call-done = bf16[21,16,512]{2,1,0:T(8,128)(2,1)} async-done(((bf16[21,512,512]{2,1,0:T(8,128)(2,1)}), bf16[21,16,512]{2,1,0:T(8,128)(2,1)}) %reduce-scatter.2.cloned.1.call-update) | async-done | bytes 344080 | tf_op jit(solution)/shard_map/reduce_scatter | solution.py:612
  460.1 1.0 convert_element_type.5
  461.2 0.7 slice.75
  461.8 0.1 slice.71
  461.9 0.1 slice.78
  462.0 0.6 slice.68
  462.6 0.1 fusion.2
  462.7 0.7 copy.64
  463.3 0.7 copy.65
  464.0 0.1 copy.62
  464.1 0.6 reshape.96
  464.7 0.1 copy.60
  464.8 0.6 reshape.92
  465.4 0.6 copy.63
  466.0 1.5 fusion
  467.5 0.2 reshape.94
  467.7 0.4 copy.61
  468.1 1.4 reshape.95
  469.5 0.2 reshape.90
  469.7 0.4 copy.59
  470.1 1.4 reshape.91
  471.5 1.7 fusion.1
  (7 shorter events, 0.1 us)
Async XLA Ops:
  7.2 104.7 %all-gather.2.cloned.1.call-start = ((), (), s32[]{:S(2)}) async-start(), calls=%async_computation.1 | async-start | bytes 11354112 | tf_op jit(solution)/shard_map/all_gather | solution.py:608
  19.5 0.7 copy-start
  20.3 439.8 %reduce-scatter.2.cloned.1.call-start = ((), (), s32[]{:S(2)}) async-start(), calls=%async_computation.2 | async-start | bytes 11354112 | tf_op jit(solution)/shard_map/reduce_scatter | solution.py:612
Sparse Core Ops, SparseCore 0:
  20.4 91.4 all-gather.1
  222.8 237.2 reduce-scatter.1

commit v3 on v2

v3 whole, which is shorter than its diff:
```python
from functools import partial
import math

import jax
import jax.numpy as jnp
import numpy as np
from jax import lax
from jax.experimental import pallas as pl
from jax.experimental.pallas import tpu as pltpu
from jax.sharding import PartitionSpec as P

HEADS = 8
VOCAB = 32
AXES = ("wide", "narrow")
LOW = jnp.bfloat16
WIDE = jnp.float32

MISC, ENC, ENC_IN, ENC_OUT, SELF, CROSS, DEC_IN, DEC_OUT, PIECES = 0, 1, 5, 7, 9, 13, 17, 19, 21
BITS = (2,) * 5
BLOCKS = 32
BN, AFFINE, ENC_VEC, DEC_VEC, TABLE, VECTOR_ROWS = 0, 2, 4, 9, 16, 128
E1, E2, D1, D2, D3, RD3, RD2, RD1, RE2, RA, RB = range(11)
(
    AT_ENCODE,
    AT_ENC_ATTEND,
    AT_ENC_FEED,
    AT_SELF_ATTEND,
    AT_CROSS_ATTEND,
    AT_DEC_FEED,
    AT_DEC_FFN_GRADS,
    AT_CROSS_BACK,
    AT_CROSS_END,
    AT_SELF_ROWS,
    AT_CROSS_GRADS,
    AT_SELF_BACK,
    AT_SELF_END,
    AT_SELF_GRADS,
    AT_ENC_FEED_BACK,
    AT_ENC_FFN_GRADS,
    AT_ENC_BACK,
    AT_ENC_END,
    AT_ENC_GRADS,
    AT_PROJECT_BACK,
    AT_DECODE,
) = range(21)
ENC_HIDDEN, DEC_HIDDEN = TABLE + VOCAB, TABLE + VOCAB + 2


def dot_nn(left, right):
    return lax.dot_general(left, right, (((1,), (0,)), ((), ())), preferred_element_type=WIDE)


def dot_nt(left, right):
    return lax.dot_general(left, right, (((1,), (1,)), ((), ())), preferred_element_type=WIDE)


def dot_tn(left, right):
    return lax.dot_general(left, right, (((0,), (0,)), ((), ())), preferred_element_type=WIDE)


def position_table(rows, width):
    place = np.arange(rows, dtype=np.float64)[:, None]
    column = np.arange(width)
    inverse = np.exp(-(2 * (column // 2)) / width * math.log(10000.0))
    angle = place * inverse[None, :]
    return np.where((column % 2 == 0)[None, :], np.sin(angle), np.cos(angle)).astype(np.float32)


def norm_stats(value):
    centred = value - jnp.mean(value, axis=1, keepdims=True)
    scale = lax.rsqrt(jnp.mean(centred * centred, axis=1, keepdims=True) + 1e-05)
    return centred * scale, scale


def norm_back(grad, normal, scale, gain):
    inner = grad * gain
    return scale * (
        inner
        - jnp.mean(inner, axis=1, keepdims=True)
        - normal * jnp.mean(inner * normal, axis=1, keepdims=True)
    )


def col_sum(value):
    return jnp.sum(value, axis=0, keepdims=True)


def gauss_share(value):
    return 0.5 + 0.5 * lax.erf(value * math.sqrt(0.5))


def gauss_slope(value):
    return jnp.exp(value * value * -0.5) * (1.0 / math.sqrt(2.0 * math.pi))


def two_tiles(count):
    top = (count // 2 + 15) // 16 * 16
    return [(0, top), (top, count - top)]


def pick(mask, half, value):
    zero = jnp.zeros((), value.dtype)
    return jnp.where(mask, value, zero) if half == 0 else jnp.where(mask, zero, value)


def first_half(shape):
    return lax.broadcasted_iota(jnp.int32, shape, 1) < shape[1] // 2


FAR, NEAR, SIDE, CORE, ACROSS = range(5)
DEEP = (FAR, NEAR)
ROUTES = ((DEEP, (ACROSS,), (SIDE,)), (DEEP, (SIDE,), (ACROSS,)), ((ACROSS,), (SIDE,), DEEP))


def my_place():
    wide = lax.axis_index("wide")
    return (wide // 8, wide // 4 % 2, wide // 2 % 2, wide % 2, lax.axis_index("narrow"))


def flips(axes):
    if len(axes) == 1:
        return [axes]
    return [axes[:1], axes[1:], axes]


def across(place, flip):
    return tuple(1 - p if i in flip else p for i, p in enumerate(place))


def device_at(place):
    far, near, side, core, narrow = place
    return (far * 8 + near * 4 + side * 2 + core, narrow)


def greet(place):
    for flip in flips(DEEP) + [(SIDE,), (CORE,), (ACROSS,)]:
        pl.semaphore_signal(
            pltpu.get_barrier_semaphore(),
            inc=1,
            device_id=device_at(across(place, flip)),
            device_id_type=pl.DeviceIdType.MESH,
        )


def await_greetings():
    pl.semaphore_wait(pltpu.get_barrier_semaphore(), 6)


def cube(stack, pieces, place, open_axes):
    index = tuple(slice(None) if i in open_axes else p for i, p in enumerate(place))
    return stack.at[(slice(*pieces),) + index]


class Gather:
    sems = 8

    def __init__(self, stack, place, pieces, route, sends, arrivals, base):
        self.stack, self.place, self.pieces, self.route = stack, place, pieces, route
        self.sends, self.arrivals, self.base = sends, arrivals, base

    def copy(self, which, flip, place, open_axes):
        part = cube(self.stack, self.pieces, place, open_axes)
        return pltpu.make_async_remote_copy(
            src_ref=part,
            dst_ref=part,
            send_sem=self.sends.at[self.base + which],
            recv_sem=self.arrivals.at[self.base + which],
            device_id=device_at(across(self.place, flip)),
            device_id_type=pl.DeviceIdType.MESH,
        )

    def hop(self, step):
        before = self.route[:step]
        first = sum(len(flips(axes)) for axes in before)
        held = sum(before, ())
        return [
            self.copy(first + i, flip, self.place, held)
            for i, flip in enumerate(flips(self.route[step]))
        ]

    def hand(self, last):
        held = self.route[0] + self.route[1]
        if not last:
            return [self.copy(4 + len(flips(self.route[2])), (CORE,), self.place, held)]
        return [
            self.copy(5 + len(flips(self.route[2])) + i, (CORE,), across(self.place, flip), held)
            for i, flip in enumerate(flips(self.route[2]))
        ]

    def advance(self, step):
        if step:
            for copy in self.hop(step - 1):
                copy.wait_recv()
        if step < 3:
            for copy in self.hop(step):
                copy.start()
        if step >= 2:
            for copy in self.hand(step == 3):
                copy.start()

    def finish(self):
        for copy in self.hand(False) + self.hand(True):
            copy.wait_recv()

    def drain(self):
        for copy in sum([self.hop(step) for step in range(3)], []) + self.hand(False) + self.hand(True):
            copy.wait_send()


class Scatter:
    sems = 6

    def __init__(self, stack, place, slots, route, inbox, room, share, piece, sends, arrivals, base):
        self.stack, self.place, self.slots, self.piece = stack, place, slots, piece
        self.order = ((CORE,),) + tuple(reversed(route))
        self.inbox, self.room, self.share = inbox, room, share
        self.sends, self.arrivals, self.base = sends, arrivals, base

    def open_axes(self, step):
        return [a for a in range(5) if a not in sum(self.order[: step + 1], ())]

    def hop(self, step):
        first = sum(len(flips(axes)) for axes in self.order[:step])
        count = self.slots[1] - self.slots[0]
        return [
            pltpu.make_async_remote_copy(
                src_ref=cube(self.stack, self.slots, across(self.place, flip), self.open_axes(step)),
                dst_ref=self.inbox[step].at[i, self.room : self.room + count],
                send_sem=self.sends.at[self.base + first + i],
                recv_sem=self.arrivals.at[self.base + first + i],
                device_id=device_at(across(self.place, flip)),
                device_id_type=pl.DeviceIdType.MESH,
            )
            for i, flip in enumerate(flips(self.order[step]))
        ]

    def advance(self, step):
        if step:
            for copy in self.hop(step - 1):
                copy.wait_recv()
            self.add(step - 1)
        if step < 4:
            for copy in self.hop(step):
                copy.start()
        else:
            self.drain()

    def add(self, step):
        first = self.slots[0]
        for at in range(self.slots[1] - first):
            mine = cube(self.stack, (first + at, first + at + 1), self.place, self.open_axes(step))
            total = mine[...][0].astype(WIDE)
            for i in range(len(flips(self.order[step]))):
                total = total + self.inbox[step][i, self.room + at].astype(WIDE)
            if step < 3:
                mine[...] = total.astype(mine.dtype)[None]
            else:
                self.share[self.piece + at] = total

    def drain(self):
        for step in range(4):
            for copy in self.hop(step):
                copy.wait_send()


def inbox_shapes(count, route, rows, width):
    order, left, shapes = ((CORE,),) + tuple(reversed(route)), 5, []
    for axes in order:
        left -= len(axes)
        shapes.append((len(flips(axes)), count) + (2,) * left + (rows, width))
    return shapes


class Group:
    def __init__(self, runs):
        self.runs = runs

    def advance(self, step):
        for run in self.runs:
            run.advance(step)

    def finish(self):
        for run in self.runs:
            run.finish()

    def drain(self):
        for run in self.runs:
            run.drain()


def run_tick(index, ticks):
    for at, tick in enumerate(ticks):
        if tick is not None:
            pl.when(index == at)(tick)


def pair_ticks(ticks, number, count):
    return ticks[number::count]


def attend(q_ref, k_ref, v_ref, o_ref, lse_ref, tiles, length, ticks=()):
    slab = 128
    half_scale = LOW(0.125)

    def pair(index, _):
        cols = pl.ds(pl.multiple_of(index * slab, slab), slab)
        for number, (start, size, keys) in enumerate(tiles):
            run_tick(index, pair_ticks(ticks, number, len(tiles)))
            rows = pl.ds(start, size)
            k = k_ref[0:keys, cols]
            v = v_ref[0:keys, cols]
            left_k = first_half(v.shape)
            q = q_ref[rows, cols] * half_scale
            left = first_half(q.shape)
            outs, tops, sums = [], [], []
            for half in range(2):
                s = dot_nt(pick(left, half, q), k)
                if length is not None:
                    s = mask_scores(s, start, length)
                top = jnp.max(s, axis=1, keepdims=True)
                p = jnp.exp(s - top).astype(LOW)
                ones = jnp.ones((), LOW)
                full = jnp.where(left_k, v, ones) if half == 0 else jnp.where(left_k, ones, v)
                out = dot_nn(p, full)
                outs.append(out)
                tops.append(top)
                sums.append(out[:, 64:65] if half == 0 else out[:, 0:1])
            o_ref[rows, cols] = jnp.where(left, outs[0] / sums[0], outs[1] / sums[1]).astype(LOW)
            lane = lax.broadcasted_iota(jnp.int32, (size, slab), 1) - 2 * index
            kept = jnp.where(lane == 0, tops[0] + jnp.log(sums[0]), lse_ref[rows, :])
            lse_ref[rows, :] = jnp.where(lane == 1, tops[1] + jnp.log(sums[1]), kept)
        return 0

    lax.fori_loop(0, HEADS // 2, pair, 0)


def mask_scores(s, start, length):
    query = lax.broadcasted_iota(jnp.int32, s.shape, 0) + start
    key = lax.broadcasted_iota(jnp.int32, s.shape, 1)
    return jnp.where((key <= query) & (key < length), s, -1e30)


def attend_back(
    q_ref, k_ref, v_ref, lse_ref, do_ref, dq_ref, dk_ref, dv_ref, dk_acc, dv_acc, tiles, length, ticks=()
):
    slab = 128
    half_scale = LOW(0.125)
    total = k_ref.shape[0]

    def pair(index, _):
        cols = pl.ds(pl.multiple_of(index * slab, slab), slab)
        first = True
        for number, (start, size, keys) in enumerate(sorted(tiles, key=lambda t: -t[2])):
            run_tick(index, pair_ticks(ticks, number, len(tiles)))
            rows = pl.ds(start, size)
            k = k_ref[0:keys, cols]
            v = v_ref[0:keys, cols]
            q = q_ref[rows, cols] * half_scale
            do = do_ref[rows, cols]
            lane = lax.broadcasted_iota(jnp.int32, (size, slab), 1) - 2 * index
            left = first_half(q.shape)
            grads, dks, dvs = [], [], []
            for half in range(2):
                qh, doh = pick(left, half, q), pick(left, half, do)
                s = dot_nt(qh, k)
                if length is not None:
                    s = mask_scores(s, start, length)
                lse = jnp.sum(jnp.where(lane == half, lse_ref[rows, :], 0.0), axis=1, keepdims=True)
                p = jnp.exp(s - lse)
                mixed = p * dot_nt(doh, v)
                ds = (mixed - p * jnp.sum(mixed, axis=1, keepdims=True)).astype(LOW)
                p = p.astype(LOW)
                grads.append(dot_nn(ds, k))
                dks.append(dot_tn(qh, ds))
                dvs.append(dot_tn(doh, p))
            dq_ref[rows, cols] = (jnp.where(left, grads[0], grads[1]) * 0.125).astype(LOW)
            if first:
                dk_acc[:, 0:keys] = dks[0] + dks[1]
                dv_acc[:, 0:keys] = dvs[0] + dvs[1]
            else:
                dk_acc[:, 0:keys] += dks[0] + dks[1]
                dv_acc[:, 0:keys] += dvs[0] + dvs[1]
            first = False
        dk_ref[0:total, cols] = dk_acc[:, 0:total].T.astype(LOW)
        dv_ref[0:total, cols] = dv_acc[:, 0:total].T.astype(LOW)
        return 0

    lax.fori_loop(0, HEADS // 2, pair, 0)


def layer_math(feat, ids, length, cot, w, decoded, gfeat, put, net, bufs):
    (
        x, xl, q, k, v, o, lse, r2, ml, e, el, qs, ks, vs, os, lses, s2, sl, qc, kc, vc, oc, lsec,
        fl, hid, gl, do, dq, dk, dv, dm, dk_acc, dv_acc, vec, gvec, gbias, done,
    ) = bufs
    patches, width = x.shape
    tags = e.shape[0]
    channels = feat.shape[1]
    wide_tiles = two_tiles(patches)
    tag_tiles = two_tiles(tags)
    tag_rows = slice(0, tags)

    def whole(piece):
        return w[piece].reshape(width, width)

    def out_half(piece, half):
        first, second = (w[piece + i, half].reshape(16, 16, width) for i in range(2))
        return jnp.stack([first, second], axis=1).reshape(width, width)

    def put_out(piece, half, value):
        value = value.reshape((2,) * 4 + (2, 16, width))
        for i in range(2):
            put(piece + i, half, value[:, :, :, :, i])

    def row(index):
        return vec[index : index + 1, :]

    def same(shape, left, right):
        at = [lax.broadcasted_iota(jnp.int32, shape, axis) for axis in range(2)]
        return jnp.where(left(at[0]) == right(at[1]), 1.0, 0.0).astype(LOW)

    block_of = same((width, BLOCKS), lambda r: r // 16, lambda d: d)
    quarters = [same((8, BLOCKS), lambda g, i=i: 4 * g + i, lambda d: d) for i in range(4)]
    spots = [same((BLOCKS, 128), lambda u, i=i: 32 * i + u, lambda lane: lane) for i in range(4)]

    def natural_bias(columns, first):
        r = lax.broadcasted_iota(jnp.int32, (width, BLOCKS), 0)
        u = lax.broadcasted_iota(jnp.int32, (width, BLOCKS), 1)
        own = jnp.where(u < 16, columns[:, first : first + 1], columns[:, first + 1 : first + 2])
        blocks = dot_tn(block_of, jnp.where(r % 16 == u % 16, own, 0.0).astype(LOW)).astype(LOW)
        packed = sum(
            dot_nn(dot_nn(quarters[i], blocks).astype(LOW), spots[i]) for i in range(4)
        )
        return [
            jnp.concatenate([packed[4 * half + i : 4 * half + i + 1] for i in range(4)], axis=1)
            for half in range(2)
        ]

    def bias_columns(total):
        packed = jnp.concatenate([total[:, 128 * g : 128 * (g + 1)] for g in range(8)], axis=0)
        columns = 0.0
        for part in range(2):
            low = packed.astype(LOW)
            packed = packed - low.astype(WIDE)
            blocks = sum(
                dot_tn(quarters[i], dot_nt(low, spots[i]).astype(LOW)) for i in range(4)
            )
            columns = columns + dot_nn(block_of, blocks.astype(LOW))
        r = lax.broadcasted_iota(jnp.int32, (width, BLOCKS), 0)
        u = lax.broadcasted_iota(jnp.int32, (width, BLOCKS), 1)
        return [
            jnp.sum(jnp.where(u == r % 16 + 16 * i, columns, 0.0), axis=1, keepdims=True)
            for i in range(2)
        ]

    def count_up(index, value):
        gvec[index : index + 1, :] += col_sum(value)

    net.fence(E1)
    columns = whole(MISC)[:, channels : channels + VECTOR_ROWS].astype(WIDE)
    vec[...] = columns.T
    gvec[...] = jnp.zeros_like(gvec)
    gbias[...] = jnp.zeros_like(gbias)
    enc_bias = natural_bias(columns, ENC_HIDDEN)
    dec_bias = natural_bias(columns, DEC_HIDDEN)
    bn_scale = lax.rsqrt(row(BN + 1) + 1e-05)
    project = whole(MISC)[:, 0:channels]

    for number, (start, size) in enumerate(wide_tiles):
        rows = pl.ds(start, size)
        projected = dot_nt(feat[rows, :], project)
        begin = (projected - row(BN)) * bn_scale * row(AFFINE) + row(AFFINE + 1) + dm[rows, :]
        x[rows, :] = begin
        low = begin.astype(LOW)
        xl[rows, :] = low
        q[rows, :] = dot_nn(low, whole(ENC)).astype(LOW)
        k[rows, :] = dot_nn(low, whole(ENC + 1)).astype(LOW)
        v[rows, :] = dot_nn(low, whole(ENC + 2)).astype(LOW)
        net.tick(AT_ENCODE, number)
    attend(q, k, v, o, lse, [(0, patches, patches)], None, net.ticks(AT_ENC_ATTEND))
    net.fence(E2)

    for number, (start, size) in enumerate(wide_tiles):
        rows = pl.ds(start, size)
        resid = x[rows, :] + dot_nn(o[rows, :], whole(ENC + 3))
        x[rows, :] = resid
        normal, _scale = norm_stats(resid)
        first = normal * row(ENC_VEC) + row(ENC_VEC + 1)
        low = first.astype(LOW)
        total = first + row(ENC_VEC + 2)
        for half in range(2):
            pre = dot_nn(low, whole(ENC_IN + half)) + enc_bias[half]
            act = (pre * gauss_share(pre)).astype(LOW)
            total = total + dot_nn(act, out_half(ENC_OUT, half))
        r2[rows, :] = total
        normal, _scale = norm_stats(total)
        ml[rows, :] = (normal * row(ENC_VEC + 3) + row(ENC_VEC + 4)).astype(LOW)
        net.tick(AT_ENC_FEED, number)
    net.fence(D1)

    onehot = (
        lax.broadcasted_iota(jnp.int32, (VOCAB, tags), 0) == ids[0:1, :]
    ).astype(WIDE).astype(LOW)
    table = vec[TABLE : TABLE + VOCAB, :].astype(LOW)
    e[...] = dot_tn(onehot, table) + dm[0:tags, :]
    el[...] = e[...].astype(LOW)
    qs[...] = dot_nn(el[...], whole(SELF)).astype(LOW)
    ks[...] = dot_nn(el[...], whole(SELF + 1)).astype(LOW)
    vs[...] = dot_nn(el[...], whole(SELF + 2)).astype(LOW)
    causal_tiles = [(start, size, start + size) for start, size in tag_tiles]
    attend(qs, ks, vs, os, lses, causal_tiles, length, net.ticks(AT_SELF_ATTEND))
    net.fence(D2)

    for start, size in tag_tiles:
        rows = pl.ds(start, size)
        resid = e[rows, :] + dot_nn(os[rows, :], whole(SELF + 3))
        e[rows, :] = resid
        normal, _scale = norm_stats(resid)
        second = normal * row(DEC_VEC) + row(DEC_VEC + 1)
        s2[rows, :] = second
        sl[rows, :] = second.astype(LOW)
        qc[rows, :] = dot_nn(sl[rows, :], whole(CROSS)).astype(LOW)
    kc[...] = dot_nn(ml[...], whole(CROSS + 1)).astype(LOW)
    vc[...] = dot_nn(ml[...], whole(CROSS + 2)).astype(LOW)
    net.tick(AT_DECODE, 0)
    attend(qc, kc, vc, oc, lsec, [(0, tags, patches)], None, net.ticks(AT_CROSS_ATTEND))
    net.fence(D3)

    for number, (start, size) in enumerate(tag_tiles):
        rows = pl.ds(start, size)
        resid = s2[rows, :] + dot_nn(oc[rows, :], whole(CROSS + 3))
        normal_two, scale_two = norm_stats(resid)
        third = normal_two * row(DEC_VEC + 2) + row(DEC_VEC + 3)
        low = third.astype(LOW)
        fl[rows, :] = low
        total = third + row(DEC_VEC + 4)
        kept = []
        for half in range(2):
            pre = dot_nn(low, whole(DEC_IN + half)) + dec_bias[half]
            share = gauss_share(pre)
            act = (pre * share).astype(LOW)
            hid[rows, half * width : (half + 1) * width] = act
            total = total + dot_nn(act, out_half(DEC_OUT, half))
            kept.append(share + pre * gauss_slope(pre))
        normal, scale = norm_stats(total)
        place = lax.broadcasted_iota(jnp.int32, (size, 1), 0) + start
        live = jnp.where(place < length, 1.0, 0.0)
        decoded[rows, :] = ((normal * row(DEC_VEC + 5) + row(DEC_VEC + 6)) * live).astype(LOW)
        grad = cot[rows, :].astype(WIDE) * live
        count_up(DEC_VEC + 5, grad * normal)
        count_up(DEC_VEC + 6, grad)
        grad = norm_back(grad, normal, scale, row(DEC_VEC + 5))
        count_up(DEC_VEC + 4, grad)
        grad_low = grad.astype(LOW)
        gl[rows, :] = grad_low
        for half in range(2):
            back = dot_nt(grad_low, out_half(DEC_OUT, half)) * kept[half]
            gbias[1:2, half * width : (half + 1) * width] += col_sum(back)
            back = back.astype(LOW)
            (dk, dv)[half][rows, :] = back
            grad = grad + dot_nt(back, whole(DEC_IN + half))
        count_up(DEC_VEC + 2, grad * normal_two)
        count_up(DEC_VEC + 3, grad)
        grad = norm_back(grad, normal_two, scale_two, row(DEC_VEC + 2))
        s2[rows, :] = grad
        dq[rows, :] = grad.astype(LOW)
        do[rows, :] = dot_nt(dq[rows, :], whole(CROSS + 3)).astype(LOW)
        net.tick(AT_DEC_FEED, number)

    def weight_grad(piece, left, right):
        put(piece, None, dot_tn(left, right))

    for half in range(2):
        cols = slice(half * width, (half + 1) * width)
        weight_grad(DEC_IN + half, fl[tag_rows, :], (dk, dv)[half][tag_rows, :])
        put_out(DEC_OUT, half, dot_tn(hid[tag_rows, cols], gl[tag_rows, :]))
    net.tick(AT_DEC_FFN_GRADS, 0)
    weight_grad(CROSS + 3, oc[...], dq[tag_rows, :])
    attend_back(
        qc, kc, vc, lsec, do, dq, dk, dv, dk_acc, dv_acc, [(0, tags, patches)], None,
        net.ticks(AT_CROSS_BACK),
    )
    net.tick(AT_CROSS_END, 0)
    for start, size in wide_tiles:
        rows = pl.ds(start, size)
        dm[rows, :] = dot_nt(dk[rows, :], whole(CROSS + 1)) + dot_nt(dv[rows, :], whole(CROSS + 2))
    for start, size in tag_tiles:
        rows = pl.ds(start, size)
        grad = s2[rows, :] + dot_nt(dq[rows, :], whole(CROSS))
        normal, scale = norm_stats(e[rows, :])
        count_up(DEC_VEC, grad * normal)
        count_up(DEC_VEC + 1, grad)
        grad = norm_back(grad, normal, scale, row(DEC_VEC))
        s2[rows, :] = grad
        gl[rows, :] = grad.astype(LOW)
        do[rows, :] = dot_nt(gl[rows, :], whole(SELF + 3)).astype(LOW)
    net.tick(AT_SELF_ROWS, 0)
    weight_grad(CROSS, sl[...], dq[tag_rows, :])
    weight_grad(CROSS + 1, ml[...], dk[...])
    weight_grad(CROSS + 2, ml[...], dv[...])
    net.tick(AT_CROSS_GRADS, 0)
    weight_grad(SELF + 3, os[...], gl[tag_rows, :])
    attend_back(
        qs, ks, vs, lses, do, dq, dk, dv, dk_acc, dv_acc, causal_tiles, length,
        net.ticks(AT_SELF_BACK),
    )
    net.tick(AT_SELF_END, 0)
    grad = (
        s2[...]
        + dot_nt(dq[tag_rows, :], whole(SELF))
        + dot_nt(dk[tag_rows, :], whole(SELF + 1))
        + dot_nt(dv[tag_rows, :], whole(SELF + 2))
    )
    high = grad.astype(LOW)
    rest = (grad - high.astype(WIDE)).astype(LOW)
    gvec[TABLE : TABLE + VOCAB, :] = dot_nn(onehot, high) + dot_nn(onehot, rest)
    weight_grad(SELF, el[...], dq[tag_rows, :])
    weight_grad(SELF + 1, el[...], dk[tag_rows, :])
    weight_grad(SELF + 2, el[...], dv[tag_rows, :])
    net.tick(AT_SELF_GRADS, 0)

    for number, (start, size) in enumerate(wide_tiles):
        rows = pl.ds(start, size)
        normal, scale = norm_stats(r2[rows, :])
        grad = dm[rows, :]
        count_up(ENC_VEC + 3, grad * normal)
        count_up(ENC_VEC + 4, grad)
        grad = norm_back(grad, normal, scale, row(ENC_VEC + 3))
        count_up(ENC_VEC + 2, grad)
        grad_low = grad.astype(LOW)
        gl[rows, :] = grad_low
        normal, scale = norm_stats(x[rows, :])
        low = (normal * row(ENC_VEC) + row(ENC_VEC + 1)).astype(LOW)
        fl[rows, :] = low
        for half in range(2):
            cols = slice(half * width, (half + 1) * width)
            pre = dot_nn(low, whole(ENC_IN + half)) + enc_bias[half]
            share = gauss_share(pre)
            (kc, vc)[half][rows, :] = (pre * share).astype(LOW)
            back = dot_nt(grad_low, out_half(ENC_OUT, half)) * (share + pre * gauss_slope(pre))
            gbias[0:1, cols] += col_sum(back)
            back = back.astype(LOW)
            (dk, dv)[half][rows, :] = back
            grad = grad + dot_nt(back, whole(ENC_IN + half))
        count_up(ENC_VEC, grad * normal)
        count_up(ENC_VEC + 1, grad)
        grad = norm_back(grad, normal, scale, row(ENC_VEC))
        dm[rows, :] = grad
        dq[rows, :] = grad.astype(LOW)
        do[rows, :] = dot_nt(dq[rows, :], whole(ENC + 3)).astype(LOW)
        net.tick(AT_ENC_FEED_BACK, number)
    for half in range(2):
        weight_grad(ENC_IN + half, fl[...], (dk, dv)[half][...])
        put_out(ENC_OUT, half, dot_tn((kc, vc)[half][...], gl[...]))
    weight_grad(ENC + 3, o[...], dq[...])
    net.tick(AT_ENC_FFN_GRADS, 0)
    halves = [(start, size, patches) for start, size in wide_tiles]
    attend_back(
        q, k, v, lse, do, dq, dk, dv, dk_acc, dv_acc, halves, None, net.ticks(AT_ENC_BACK)
    )
    net.tick(AT_ENC_END, 0)
    weight_grad(ENC, xl[...], dq[...])
    weight_grad(ENC + 1, xl[...], dk[...])
    weight_grad(ENC + 2, xl[...], dv[...])
    net.tick(AT_ENC_GRADS, 0)
    for number, (start, size) in enumerate(wide_tiles):
        rows = pl.ds(start, size)
        grad = (
            dm[rows, :]
            + dot_nt(dq[rows, :], whole(ENC))
            + dot_nt(dk[rows, :], whole(ENC + 1))
            + dot_nt(dv[rows, :], whole(ENC + 2))
        )
        projected = dot_nt(feat[rows, :], project)
        count_up(AFFINE, grad * (projected - row(BN)) * bn_scale)
        count_up(AFFINE + 1, grad)
        low = (grad * (bn_scale * row(AFFINE))).astype(LOW)
        gl[rows, :] = low
        r2[rows, 0:channels] = dot_nn(low, project)
        net.tick(AT_PROJECT_BACK, number)
    out = pltpu.make_async_copy(r2.at[:, 0:channels], gfeat, done)
    out.start()
    columns = gvec[...].T
    lane = lax.broadcasted_iota(jnp.int32, columns.shape, 1)
    for index, first in ((0, ENC_HIDDEN), (1, DEC_HIDDEN)):
        for i, column in enumerate(bias_columns(gbias[index : index + 1, :])):
            columns = jnp.where(lane == first + i, column, columns)
    put(
        MISC,
        None,
        jnp.concatenate(
            [
                dot_tn(gl[...], feat[...]),
                columns,
                jnp.zeros((width, width - channels - VECTOR_ROWS), WIDE),
            ],
            axis=1,
        ),
    )
    net.flush()
    out.wait()


def math_buffers(patches, tags, width, hidden):
    wide = lambda *shape: pltpu.VMEM(shape, WIDE)
    low = lambda *shape: pltpu.VMEM(shape, LOW)
    rows, slots = (patches, width), (tags, width)
    return [
        wide(*rows), low(*rows), low(*rows), low(*rows), low(*rows), low(*rows), wide(patches, 128),
        wide(*rows), low(*rows),
        wide(*slots), low(*slots), low(*slots), low(*slots), low(*slots), low(*slots), wide(tags, 128),
        wide(*slots), low(*slots), low(*slots), low(*rows), low(*rows), low(*slots), wide(tags, 128),
        low(*rows), low(tags, hidden), low(*rows),
        low(*rows), low(*rows), low(*rows), low(*rows), wide(*rows),
        wide(128, patches), wide(128, patches), wide(VECTOR_ROWS, width), wide(VECTOR_ROWS, width),
        wide(8, hidden), pltpu.SemaphoreType.DMA(()),
    ]


class Quiet:
    def tick(self, name, number):
        pass

    def ticks(self, name):
        return ()

    def fence(self, name):
        pass

    def flush(self):
        pass


LAST = 9
HEAD = (
    ((E1, 0),),
    ((E1, 1), (E2, 0)),
    ((E1, 2), (D1, 0)),
    ((E1, 3), (E2, 1)),
)
PLAN = {
    (AT_ENCODE, 1): ((E2, 2), (D2, 0)),
    (AT_ENC_ATTEND, 1): ((D1, 1),),
    (AT_ENC_ATTEND, 2): ((E2, 3), (D3, 0)),
    (AT_ENC_ATTEND, 3): ((D1, 2), (D2, 1)),
    (AT_ENC_FEED, 0): ((D2, 2), (D3, 1)),
    (AT_ENC_FEED, 1): ((D1, 3),),
    (AT_SELF_ATTEND, 4): ((D3, 2),),
    (AT_SELF_ATTEND, 7): ((D2, 3),),
    (AT_CROSS_ATTEND, 2): ((D3, 3), (D2, LAST)),
    (AT_DEC_FEED, 1): ((D3, LAST),),
    (AT_DEC_FFN_GRADS, 0): ((RD3, 0),),
    (AT_CROSS_BACK, 1): ((RD3, 1),),
    (AT_CROSS_END, 0): ((RD3, 2), (D1, LAST)),
    (AT_CROSS_GRADS, 0): ((RD3, 3), (RD2, 0)),
    (AT_SELF_BACK, 4): ((RD2, 1),),
    (AT_SELF_END, 0): ((RD3, 4),),
    (AT_SELF_GRADS, 0): ((RD1, 0),),
    (AT_ENC_FEED_BACK, 0): ((RD2, 2),),
    (AT_ENC_FEED_BACK, 1): ((RD1, 1), (E1, LAST), (E2, LAST)),
    (AT_ENC_FFN_GRADS, 0): ((RD2, 3), (RE2, 0)),
    (AT_ENC_BACK, 2): ((RD1, 2),),
    (AT_ENC_BACK, 3): ((RD2, 4), (RE2, 1)),
    (AT_ENC_BACK, 4): ((RD1, 3),),
    (AT_ENC_BACK, 6): ((RE2, 2),),
    (AT_ENC_BACK, 7): ((RD1, 4),),
    (AT_ENC_END, 0): ((RE2, 3),),
    (AT_ENC_GRADS, 0): ((RA, 0),),
    (AT_PROJECT_BACK, 1): ((RE2, 4), (RA, 1)),
}
TAIL = (
    ((RB, 0),),
    ((RA, 2), (RB, 1)),
    ((RA, 3), (RB, 2)),
    ((RA, 4), (RB, 3)),
    ((RB, 4),),
)
GATHERS = {
    E1: ((MISC, 2, 0), (MISC + 2, 2, 1)),
    E2: ((ENC + 3, 3, 0), (ENC + 6, 2, 1)),
    D1: ((SELF, 2, 0), (SELF + 2, 2, 1)),
    D2: ((CROSS, 2, 0), (CROSS + 2, 2, 1)),
    D3: ((DEC_IN, 2, 0), (DEC_OUT, 2, 1)),
}
SCATTERS = {
    RD3: ((DEC_IN, DEC_IN, 2, 0, 0, 0), (DEC_OUT, DEC_OUT, 2, 1, 1, 0)),
    RD2: ((CROSS, CROSS, 2, 0, 2, 0), (CROSS + 2, CROSS + 2, 2, 1, 3, 0)),
    RD1: ((SELF, SELF, 2, 0, 4, 0), (SELF + 2, SELF + 2, 2, 1, 5, 0)),
    RE2: ((ENC + 3, ENC + 3, 3, 0, 0, 0), (ENC + 6, ENC + 6, 2, 1, 1, 0)),
    RA: ((SELF, ENC, 2, 0, 2, 0), (SELF + 2, ENC + 2, 1, 1, 3, 0)),
    RB: ((MISC, MISC, 1, 1, 3, 1),),
}
INBOX = (3, 2, 2, 2, 2, 2)


class Traffic:
    def __init__(self, place, w, inboxes, share, sems):
        gather_out, gather_in, scatter_out, scatter_in = sems
        self.groups, base = {}, 0
        for name, runs in GATHERS.items():
            self.groups[name] = Group([])
            for first, count, route in runs:
                pieces = (first, first + count)
                self.groups[name].runs.append(
                    Gather(w, place, pieces, ROUTES[route], gather_out, gather_in, base)
                )
                base += Gather.sems
        base = 0
        for name, runs in SCATTERS.items():
            self.groups[name] = Group([])
            for slot, piece, count, route, inbox, room in runs:
                self.groups[name].runs.append(
                    Scatter(
                        w, place, (slot, slot + count), ROUTES[route], inboxes[inbox], room, share, piece,
                        scatter_out, scatter_in, base,
                    )
                )
                base += Scatter.sems

    def run(self, steps):
        for name, step in steps:
            if step == LAST:
                self.groups[name].drain()
            else:
                self.groups[name].advance(step)

    def tick(self, name, number):
        self.run(PLAN.get((name, number), ()))

    def ticks(self, name):
        plans = [PLAN.get((name, number)) for number in range(HEADS)]
        return tuple(partial(self.run, plan) if plan else None for plan in plans)

    def fence(self, name):
        self.groups[name].finish()

    def flush(self):
        for plan in TAIL:
            self.run(plan)


POS_AT = 7


def fused_kernel(
    feat, ids, lens, cot, pos, proj, bn_given, bn_affine, enc_attn, enc_vec, enc_in, enc_hidden, enc_out,
    table, dec_self, dec_cross, dec_vec, dec_in, dec_hidden, dec_out, decoded, gfeat, share, *scratch
):
    w, cols, turned = scratch[:3]
    boxes = 3 + 4 * len(INBOX)
    inboxes = [scratch[3 + 4 * i : 7 + 4 * i] for i in range(len(INBOX))]
    sems, bufs = scratch[boxes : boxes + 5], scratch[boxes + 5 :]
    place = my_place()
    greet(place)
    width = w.shape[-1]
    rows = w.shape[-2]
    local = sems[0]
    channels = proj.shape[1]

    def own(first, count=1):
        return cube(w, (first, first + count), place, ())

    copies = [(enc_attn, own(ENC, 4)), (dec_self, own(SELF, 4)), (dec_cross, own(CROSS, 4))]
    for matrix, first in ((enc_in, ENC_IN), (dec_in, DEC_IN)):
        copies += [
            (matrix.at[:, half * width : (half + 1) * width], own(first + half).at[0])
            for half in range(2)
        ]
    for matrix, first in ((enc_out, ENC_OUT), (dec_out, DEC_OUT)):
        copies += [
            (matrix.at[half * rows : (half + 1) * rows, :], own(first + half).at[0])
            for half in range(2)
        ]
    copies = [
        pltpu.make_async_copy(source, target, local.at[number])
        for number, (source, target) in enumerate(copies)
    ]
    for copy in copies:
        copy.start()
    fetch = pltpu.make_async_copy(pos, bufs[-POS_AT], local.at[11])
    fetch.start()
    cols[...] = jnp.zeros_like(cols)
    for part, first in ((bn_given, BN), (bn_affine, AFFINE), (enc_vec, ENC_VEC), (dec_vec, DEC_VEC)):
        cols[first : first + part.shape[0], 0:rows] = part[...].astype(WIDE)
    for part, first in ((enc_hidden, ENC_HIDDEN), (dec_hidden, DEC_HIDDEN)):
        for half in range(2):
            cols[first + half : first + half + 1, 0:rows] = part[0:1, half * rows : (half + 1) * rows].astype(WIDE)
    turned[...] = cols[...].T[0:rows, :]
    turned[:, TABLE : TABLE + VOCAB] = table[...].astype(WIDE)
    first = jnp.concatenate(
        [proj[...], turned[...].astype(LOW), jnp.zeros((rows, width - channels - VECTOR_ROWS), LOW)], axis=1
    )
    own(MISC)[...] = first[None]
    await_greetings()
    for copy in copies:
        copy.wait()
    net = Traffic(place, w, inboxes, share, sems[1:])
    for plan in HEAD:
        net.run(plan)

    def put(piece, half, value):
        slot = piece - ENC + SELF if ENC <= piece < ENC + 3 else piece
        if half is None:
            w[slot] = value.reshape(BITS + (rows, width)).astype(LOW)
        else:
            w[slot, half] = value.reshape(BITS[1:] + (rows, width)).astype(LOW)

    fetch.wait()
    layer_math(feat, ids, lens[0], cot, w, decoded, gfeat, put, net, bufs)


def plain_kernel(feat, ids, lens, cot, pos, w, decoded, gfeat, g, *bufs):
    width = w.shape[-1]

    def put(piece, half, value):
        if half is None:
            g[piece] = value.reshape(g.shape[1:]).astype(LOW)
        else:
            g[piece, half] = value.reshape(g.shape[2:]).astype(LOW)

    pltpu.sync_copy(pos, bufs[-POS_AT])
    layer_math(feat, ids, lens[0], cot, w, decoded, gfeat, put, Quiet(), bufs)


VMEM = pl.BlockSpec(memory_space=pltpu.VMEM)
SMEM = pl.BlockSpec(memory_space=pltpu.SMEM)
ANY = pl.BlockSpec(memory_space=pl.ANY)
LIMIT = 63 << 20


def split_update(features, tag_ids, tag_lengths, out_cot, parameters):
    (
        proj, bn_given, bn_affine, enc_attn, enc_vec, enc_in, enc_hidden, enc_out,
        table, dec_self, dec_cross, dec_vec, dec_in, dec_hidden, dec_out,
    ) = parameters
    patches, channels = features.shape[1:]
    tags, width = out_cot.shape[1:]
    rows = width // BLOCKS
    pos = jnp.asarray(position_table(max(patches, tags), width))
    sems = (
        Gather.sems * sum(len(runs) for runs in GATHERS.values()),
        Scatter.sems * sum(len(runs) for runs in SCATTERS.values()),
    )
    boxes = [
        pltpu.VMEM(shape, LOW)
        for number, count in enumerate(INBOX)
        for shape in inbox_shapes(count, ROUTES[number % 2], rows, width)
    ]
    dma = pltpu.SemaphoreType.DMA
    decoded, gfeat, share = pl.pallas_call(
        fused_kernel,
        in_specs=[VMEM, VMEM, SMEM, VMEM, ANY, VMEM, VMEM, VMEM, ANY, VMEM, ANY, VMEM, ANY]
        + [VMEM, ANY, ANY, VMEM, ANY, VMEM, ANY],
        out_shape=(
            jax.ShapeDtypeStruct((tags, width), LOW),
            jax.ShapeDtypeStruct((patches, channels), WIDE),
            jax.ShapeDtypeStruct((PIECES, rows, width), WIDE),
        ),
        out_specs=(VMEM, ANY, VMEM),
        scratch_shapes=[
            pltpu.VMEM((PIECES,) + BITS + (rows, width), LOW),
            pltpu.VMEM((VECTOR_ROWS, 128), WIDE),
            pltpu.VMEM((rows, VECTOR_ROWS), WIDE),
            *boxes,
            dma((12,)),
            dma((sems[0],)),
            dma((sems[0],)),
            dma((sems[1],)),
            dma((sems[1],)),
            *math_buffers(patches, tags, width, enc_in.shape[1]),
        ],
        compiler_params=pltpu.CompilerParams(
            collective_id=0, has_side_effects=True, vmem_limit_bytes=LIMIT
        ),
        name="layers",
    )(
        features[0], tag_ids, tag_lengths, out_cot[0], pos, proj.T, bn_given, bn_affine, enc_attn, enc_vec,
        enc_in, enc_hidden.reshape(1, -1), enc_out, table.T, dec_self, dec_cross, dec_vec, dec_in,
        dec_hidden.reshape(1, -1), dec_out,
    )
    outs = finish(decoded, gfeat, share, channels)
    return (
        outs[0][None],
        outs[1][None],
        outs[2].T,
        *outs[3:7],
        outs[7].reshape(-1),
        outs[8],
        outs[9].T,
        *outs[10:14],
        outs[14].reshape(-1),
        outs[15],
    )


def finish_kernel(
    decoded, gfeat, share, decoded_out, gfeat_out, proj, affine, enc_attn, enc_vec, enc_in, enc_hidden,
    enc_out, table, dec_self, dec_cross, dec_vec, dec_in, dec_hidden, dec_out
):
    rows, width = share.shape[1:]
    channels = proj.shape[1]
    decoded_out[...] = decoded[...]
    gfeat_out[...] = gfeat[...]
    enc_attn[...] = share[ENC : ENC + 4]
    dec_self[...] = share[SELF : SELF + 4]
    dec_cross[...] = share[CROSS : CROSS + 4]
    for half in range(2):
        enc_in[:, half * width : (half + 1) * width] = share[ENC_IN + half]
        dec_in[:, half * width : (half + 1) * width] = share[DEC_IN + half]
        enc_out[half * rows : (half + 1) * rows, :] = share[ENC_OUT + half]
        dec_out[half * rows : (half + 1) * rows, :] = share[DEC_OUT + half]
    columns = share[MISC]
    proj[...] = columns[:, 0:channels]
    table[...] = columns[:, channels + TABLE : channels + TABLE + VOCAB]
    vectors = jnp.concatenate(
        [columns[:, channels : channels + VECTOR_ROWS], jnp.zeros((128 - rows, VECTOR_ROWS), WIDE)],
        axis=0,
    ).T[:, 0:rows]
    for part, first in ((affine, AFFINE), (enc_vec, ENC_VEC), (dec_vec, DEC_VEC)):
        part[...] = vectors[first : first + part.shape[0]]
    for part, first in ((enc_hidden, ENC_HIDDEN), (dec_hidden, DEC_HIDDEN)):
        part[...] = jnp.concatenate([vectors[first : first + 1], vectors[first + 1 : first + 2]], axis=1)


def finish(decoded, gfeat, share, channels):
    rows, width = share.shape[1:]
    shape = lambda *dims: jax.ShapeDtypeStruct(dims, WIDE)
    return pl.pallas_call(
        finish_kernel,
        in_specs=[VMEM] * 3,
        out_shape=(
            jax.ShapeDtypeStruct(decoded.shape, decoded.dtype),
            jax.ShapeDtypeStruct(gfeat.shape, gfeat.dtype),
            shape(rows, channels),
            shape(2, rows),
            shape(4, rows, width),
            shape(5, rows),
            shape(rows, 2 * width),
            shape(1, 2 * rows),
            shape(2 * rows, width),
            shape(rows, VOCAB),
            shape(4, rows, width),
            shape(4, rows, width),
            shape(7, rows),
            shape(rows, 2 * width),
            shape(1, 2 * rows),
            shape(2 * rows, width),
        ),
        out_specs=(VMEM,) * 16,
        name="finish",
    )(decoded, gfeat, share)


def gathered_update(features, tag_ids, tag_lengths, out_cot, parameters):
    dims = (1, 1, 1, 1, 1, 0, 0, 0, 1, 1, 1, 1, 0, 0, 0)
    full = [lax.all_gather(a, AXES, axis=d, tiled=True) for a, d in zip(parameters, dims)]
    (
        proj, bn_given, bn_affine, enc_attn, enc_vec, enc_in, enc_hidden, enc_out,
        table, dec_self, dec_cross, dec_vec, dec_in, dec_hidden, dec_out,
    ) = full
    patches, channels = features.shape[1:]
    tags, width = out_cot.shape[1:]
    rows = width // BLOCKS

    def swap(matrix):
        return matrix.reshape((BLOCKS, 2, -1) + matrix.shape[1:]).swapaxes(0, 1).reshape((2, -1) + matrix.shape[1:])

    def halves(matrix):
        return jnp.stack([matrix[:, :width], matrix[:, width:]])

    columns = jnp.concatenate(
        [proj, bn_given, bn_affine, enc_vec, dec_vec, table, swap(enc_hidden), swap(dec_hidden)], axis=0
    )
    columns = jnp.pad(columns, ((0, width - columns.shape[0]), (0, 0))).T
    stack = jnp.concatenate(
        [columns[None], enc_attn, halves(enc_in), swap(enc_out), dec_self, dec_cross]
        + [halves(dec_in), swap(dec_out)],
        axis=0,
    ).reshape((PIECES,) + BITS + (rows, width))
    decoded, gfeat, grads = pl.pallas_call(
        plain_kernel,
        in_specs=[VMEM, VMEM, SMEM, VMEM, ANY, VMEM],
        out_shape=(
            jax.ShapeDtypeStruct((tags, width), LOW),
            jax.ShapeDtypeStruct((patches, channels), WIDE),
            jax.ShapeDtypeStruct(stack.shape, LOW),
        ),
        out_specs=(VMEM, ANY, VMEM),
        scratch_shapes=math_buffers(patches, tags, width, enc_in.shape[1]),
        compiler_params=pltpu.CompilerParams(vmem_limit_bytes=LIMIT),
        name="layers",
    )(features[0], tag_ids, tag_lengths, out_cot[0], jnp.asarray(position_table(max(patches, tags), width)), stack)
    grads = grads.reshape(PIECES, width, width).astype(WIDE)
    columns = grads[MISC].T
    vectors = columns[channels:]

    def join(pair):
        return pair.reshape((2, BLOCKS, -1) + pair.shape[2:]).swapaxes(0, 1).reshape((-1,) + pair.shape[2:])

    def wide(pair):
        return jnp.concatenate([pair[0], pair[1]], axis=1)

    totals = (
        (columns[:channels], 1),
        (vectors[AFFINE : AFFINE + 2], 1),
        (grads[ENC : ENC + 4], 1),
        (vectors[ENC_VEC:DEC_VEC], 1),
        (wide(grads[ENC_IN:ENC_OUT]), 0),
        (join(vectors[ENC_HIDDEN : ENC_HIDDEN + 2]), 0),
        (join(grads[ENC_OUT:SELF]), 0),
        (vectors[TABLE : TABLE + VOCAB], 1),
        (grads[SELF:CROSS], 1),
        (grads[CROSS:DEC_IN], 1),
        (vectors[DEC_VEC:TABLE], 1),
        (wide(grads[DEC_IN:DEC_OUT]), 0),
        (join(vectors[DEC_HIDDEN : DEC_HIDDEN + 2]), 0),
        (join(grads[DEC_OUT:PIECES]), 0),
    )
    return (
        decoded[None],
        gfeat[None],
        *[lax.psum_scatter(a, AXES, scatter_dimension=d, tiled=True) for a, d in totals],
    )


def body(mesh_shape, features, tag_ids, tag_lengths, out_cot, *parameters):
    update = split_update if mesh_shape == (16, 2) else gathered_update
    return update(features, tag_ids, tag_lengths, out_cot, parameters)


def solution(mesh):
    placed = (
        P(("wide", "narrow"), None, None),
        P(("wide", "narrow"), None),
        P(("wide", "narrow")),
        P(("wide", "narrow"), None, None),
        P(None, ("wide", "narrow")),
        P(None, ("wide", "narrow")),
        P(None, ("wide", "narrow")),
        P(None, ("wide", "narrow"), None),
        P(None, ("wide", "narrow")),
        P(("wide", "narrow"), None),
        P(("wide", "narrow")),
        P(("wide", "narrow"), None),
        P(None, ("wide", "narrow")),
        P(None, ("wide", "narrow"), None),
        P(None, ("wide", "narrow"), None),
        P(None, ("wide", "narrow")),
        P(("wide", "narrow"), None),
        P(("wide", "narrow")),
        P(("wide", "narrow"), None),
    )
    return jax.shard_map(
        partial(body, tuple(mesh.shape[axis] for axis in AXES)),
        mesh=mesh,
        in_specs=placed,
        out_specs=(
            P(("wide", "narrow"), None, None),
            P(("wide", "narrow"), None, None),
            P(None, ("wide", "narrow")),
            P(None, ("wide", "narrow")),
            P(None, ("wide", "narrow"), None),
            P(None, ("wide", "narrow")),
            P(("wide", "narrow"), None),
            P(("wide", "narrow")),
            P(("wide", "narrow"), None),
            P(None, ("wide", "narrow")),
            P(None, ("wide", "narrow"), None),
            P(None, ("wide", "narrow"), None),
            P(None, ("wide", "narrow")),
            P(("wide", "narrow"), None),
            P(("wide", "narrow")),
            P(("wide", "narrow"), None),
        ),
        check_vma=False,
    )
```

time: 484 us -> 187 us (0.39)
  waiting for transfers between devices: 328 us -> 0 us
  Pallas kernels: 110 us -> 183 us
  local copies, waits for them, and re-layouts: 25.6 us -> 0 us
  between operations: 15.1 us -> 1.56 us
    reduce_scatter x1 -> x0, waiting for transfers between devices: 237 us -> none  [body(): share = lax.psum_scatter(grads, AXES, scatter_dimension=1, tiled=True)]
    all_gather x1 -> x0, waiting for transfers between devices: 90.9 us -> none  [body(): stack = lax.all_gather(packed, AXES, axis=1, tiled=True)]
    pallas_call x1 -> x2, Pallas kernels: 110 us -> 183 us  [the longest x1 180 us: split_update(): pl.pallas_call(fused_kernel, in_specs=[VMEM, VMEM, SMEM, VMEM, ANY, VMEM,...]
    unnamed x16 -> x0, local copies, waits for them, and re-layouts: 9.04 us -> none
    reshape x14 -> x0, local copies, waits for them, and re-layouts: 8.67 us -> none  [the longest x2 2.8 us: whole(): return split.transpose(1, 2, 0, 3).reshape(rows, 2 * width)]
  transfers between devices with their start and end apart: 2 -> 0, of which waited for: 2 -> 0; matrix products, arithmetic and copies ran while one was open for 0% -> 0% of each run, Pallas kernels for 0% -> 0%
where the time goes in v3:
time: 187 us; the launch traced here: 185 us
  Pallas kernels  183 us (98%)
    pallas_call x1, Pallas kernels, split_update(): pl.pallas_call(fused_kernel, in_specs=[VMEM, VMEM, SMEM, VMEM, ANY, VMEM,...  180 us

profile of v3, /device:TPU:0, one launch (start us, length us, event | category | flops | bytes accessed | tf_op | source)
XLA Modules:
  0.0 184.8 jit_solution(1507364463193650751)
XLA Ops:
  1.3 180.3 %layers.1 = (bf16[512,512]{1,0:T(8,128)(2,1)}, f32[784,256]{1,0:T(8,128)}, f32[21,16,512]{2,1,0:T(8,128)}) custom-call(bf16[784,256]{1,0:T(8,128)(2,1)} %bitcast.13, s32[1,512]{1,0:T(1,128)} %ids.1, s32[1]{0:T(128)S(6)} %copy.36.lens, bf16[512,512]{1,0:T(8,128)(2,1)} %bitcast.12, f32[784,512]{1,0:T(8,128)} %constant.2.clone.pos, bf16[16,256]{1,0:T(8,128)(2,1)} %bitcast.14, ...), custom_call_target="tpu_custom_call" | custom-call | tf_op jit(solution)/shard_map/layers/pallas_call | solution.py:950
  181.6 2.9 %finish.1 = (bf16[512,512]{1,0:T(8,128)(2,1)}, f32[784,256]{1,0:T(8,128)}, f32[16,256]{1,0:T(8,128)}, f32[2,16]{1,0:T(2,128)}, f32[4,16,512]{2,1,0:T(8,128)}, /*...) custom-call(bf16[512,512]{1,0:T(8,128)(2,1)} %get-tuple-element.35.d, ...), custom_call_target="tpu_custom_call" | custom-call | tf_op jit(solution)/shard_map/finish/pallas_call | solution.py:1028

commit v4 on v3

--- a/solution.py
+++ b/solution.py
@@ -249,6 +249,9 @@
         first = self.slots[0]
         for at in range(self.slots[1] - first):
             mine = cube(self.stack, (first + at, first + at + 1), self.place, self.open_axes(step))
+            if step < 3 and len(flips(self.order[step])) == 1:
+                mine[...] = mine[...] + self.inbox[step][0, self.room + at][None]
+                continue
             total = mine[...][0].astype(WIDE)
             for i in range(len(flips(self.order[step]))):
                 total = total + self.inbox[step][i, self.room + at].astype(WIDE)
@@ -478,6 +481,19 @@
         v[rows, :] = dot_nn(low, whole(ENC + 2)).astype(LOW)
         net.tick(AT_ENCODE, number)
     attend(q, k, v, o, lse, [(0, patches, patches)], None, net.ticks(AT_ENC_ATTEND))
+    net.fence(D1)
+
+    onehot = (
+        lax.broadcasted_iota(jnp.int32, (VOCAB, tags), 0) == ids[0:1, :]
+    ).astype(WIDE).astype(LOW)
+    table = vec[TABLE : TABLE + VOCAB, :].astype(LOW)
+    e[...] = dot_tn(onehot, table) + dm[0:tags, :]
+    el[...] = e[...].astype(LOW)
+    qs[...] = dot_nn(el[...], whole(SELF)).astype(LOW)
+    ks[...] = dot_nn(el[...], whole(SELF + 1)).astype(LOW)
+    vs[...] = dot_nn(el[...], whole(SELF + 2)).astype(LOW)
+    causal_tiles = [(start, size, start + size) for start, size in tag_tiles]
+    attend(qs, ks, vs, os, lses, causal_tiles, length, net.ticks(AT_SELF_ATTEND))
     net.fence(E2)
 
     for number, (start, size) in enumerate(wide_tiles):
@@ -496,19 +512,6 @@
         normal, _scale = norm_stats(total)
         ml[rows, :] = (normal * row(ENC_VEC + 3) + row(ENC_VEC + 4)).astype(LOW)
         net.tick(AT_ENC_FEED, number)
-    net.fence(D1)
-
-    onehot = (
-        lax.broadcasted_iota(jnp.int32, (VOCAB, tags), 0) == ids[0:1, :]
-    ).astype(WIDE).astype(LOW)
-    table = vec[TABLE : TABLE + VOCAB, :].astype(LOW)
-    e[...] = dot_tn(onehot, table) + dm[0:tags, :]
-    el[...] = e[...].astype(LOW)
-    qs[...] = dot_nn(el[...], whole(SELF)).astype(LOW)
-    ks[...] = dot_nn(el[...], whole(SELF + 1)).astype(LOW)
-    vs[...] = dot_nn(el[...], whole(SELF + 2)).astype(LOW)
-    causal_tiles = [(start, size, start + size) for start, size in tag_tiles]
-    attend(qs, ks, vs, os, lses, causal_tiles, length, net.ticks(AT_SELF_ATTEND))
     net.fence(D2)
 
     for start, size in tag_tiles:
@@ -734,20 +737,22 @@
 LAST = 9
 HEAD = (
     ((E1, 0),),
-    ((E1, 1), (E2, 0)),
-    ((E1, 2), (D1, 0)),
-    ((E1, 3), (E2, 1)),
+    ((E1, 1), (D1, 0)),
+    ((E1, 2), (E2, 0)),
+    ((E1, 3), (D1, 1)),
 )
 PLAN = {
-    (AT_ENCODE, 1): ((E2, 2), (D2, 0)),
-    (AT_ENC_ATTEND, 1): ((D1, 1),),
-    (AT_ENC_ATTEND, 2): ((E2, 3), (D3, 0)),
-    (AT_ENC_ATTEND, 3): ((D1, 2), (D2, 1)),
-    (AT_ENC_FEED, 0): ((D2, 2), (D3, 1)),
-    (AT_ENC_FEED, 1): ((D1, 3),),
-    (AT_SELF_ATTEND, 4): ((D3, 2),),
-    (AT_SELF_ATTEND, 7): ((D2, 3),),
-    (AT_CROSS_ATTEND, 2): ((D3, 3), (D2, LAST)),
+    (AT_ENCODE, 1): ((D1, 2),),
+    (AT_ENC_ATTEND, 0): ((E2, 1), (D2, 0)),
+    (AT_ENC_ATTEND, 1): ((D2, 1),),
+    (AT_ENC_ATTEND, 2): ((E2, 2),),
+    (AT_ENC_ATTEND, 3): ((D1, 3), (D2, 2)),
+    (AT_SELF_ATTEND, 0): ((D3, 0),),
+    (AT_SELF_ATTEND, 5): ((E2, 3),),
+    (AT_SELF_ATTEND, 7): ((D3, 1),),
+    (AT_ENC_FEED, 0): ((D2, 3),),
+    (AT_ENC_FEED, 1): ((D3, 2),),
+    (AT_CROSS_ATTEND, 3): ((D3, 3), (D2, LAST)),
     (AT_DEC_FEED, 1): ((D3, LAST),),
     (AT_DEC_FFN_GRADS, 0): ((RD3, 0),),
     (AT_CROSS_BACK, 1): ((RD3, 1),),
@@ -787,10 +792,10 @@
     RD2: ((CROSS, CROSS, 2, 0, 2, 0), (CROSS + 2, CROSS + 2, 2, 1, 3, 0)),
     RD1: ((SELF, SELF, 2, 0, 4, 0), (SELF + 2, SELF + 2, 2, 1, 5, 0)),
     RE2: ((ENC + 3, ENC + 3, 3, 0, 0, 0), (ENC + 6, ENC + 6, 2, 1, 1, 0)),
-    RA: ((SELF, ENC, 2, 0, 2, 0), (SELF + 2, ENC + 2, 1, 1, 3, 0)),
+    RA: ((SELF, ENC, 1, 0, 2, 0), (SELF + 1, ENC + 1, 1, 1, 3, 0), (SELF + 2, ENC + 2, 1, 2, 6, 0)),
     RB: ((MISC, MISC, 1, 1, 3, 1),),
 }
-INBOX = (3, 2, 2, 2, 2, 2)
+INBOX = ((3, 0), (2, 1), (2, 0), (2, 1), (2, 0), (2, 1), (1, 2))
 
 
 class Traffic:
@@ -943,8 +948,8 @@
     )
     boxes = [
         pltpu.VMEM(shape, LOW)
-        for number, count in enumerate(INBOX)
-        for shape in inbox_shapes(count, ROUTES[number % 2], rows, width)
+        for count, route in INBOX
+        for shape in inbox_shapes(count, ROUTES[route], rows, width)
     ]
     dma = pltpu.SemaphoreType.DMA
     decoded, gfeat, share = pl.pallas_call(

time: 187 us -> 177 us (0.947)
  Pallas kernels: 183 us -> 172 us
    pallas_call x1, Pallas kernels: 180 us -> 170 us  [split_update(): pl.pallas_call(fused_kernel, in_specs=[VMEM, VMEM, SMEM, VMEM, ANY, VMEM,...]
where the time goes in v4:
time: 177 us; the launch traced here: 174 us
  Pallas kernels  172 us (97%)
    pallas_call x1, Pallas kernels, split_update(): pl.pallas_call(fused_kernel, in_specs=[VMEM, VMEM, SMEM, VMEM, ANY, VMEM,...  170 us

profile of v4, /device:TPU:0, one launch (start us, length us, event | category | flops | bytes accessed | tf_op | source)
XLA Modules:
  0.0 173.9 jit_solution(7764340432507409498)
XLA Ops:
  1.3 169.5 %layers.1 = (bf16[512,512]{1,0:T(8,128)(2,1)}, f32[784,256]{1,0:T(8,128)}, f32[21,16,512]{2,1,0:T(8,128)}) custom-call(bf16[784,256]{1,0:T(8,128)(2,1)} %bitcast.13, s32[1,512]{1,0:T(1,128)} %ids.1, s32[1]{0:T(128)S(6)} %copy.36.lens, bf16[512,512]{1,0:T(8,128)(2,1)} %bitcast.12, f32[784,512]{1,0:T(8,128)} %constant.2.clone.pos, bf16[16,256]{1,0:T(8,128)(2,1)} %bitcast.14, ...), custom_call_target="tpu_custom_call" | custom-call | tf_op jit(solution)/shard_map/layers/pallas_call | solution.py:955
  170.8 2.9 %finish.1 = (bf16[512,512]{1,0:T(8,128)(2,1)}, f32[784,256]{1,0:T(8,128)}, f32[16,256]{1,0:T(8,128)}, f32[2,16]{1,0:T(2,128)}, f32[4,16,512]{2,1,0:T(8,128)}, /*...) custom-call(bf16[512,512]{1,0:T(8,128)(2,1)} %get-tuple-element.35.d, ...), custom_call_target="tpu_custom_call" | custom-call | tf_op jit(solution)/shard_map/finish/pallas_call | solution.py:1033
